TPU v7x, 32 devices: a whole 2x2x4 slice. The times are simulated.
32 devices in a mesh: dp: 8 (over y, x, core), tensor: 4 (over z).
Axes of the slice: x: 2, y: 2, z: 4, core: 2. Of those that a mesh axis runs over, the one named last changes fastest.
Arguments:
- gate_pre: bfloat16 [4096, 14336], P('dp', 'tensor'), may hold values from -6 to 6
- up_pre: bfloat16 [4096, 14336], P('dp', 'tensor'), may hold values from -6 to 6
- grad_out: bfloat16 [4096, 4096], P(('dp', 'tensor')), may hold values from -6 to 6
- codes: bfloat16 [14336, 4096], P('tensor'), as said below
- scales: int32 [448, 4096], P('tensor'), may hold values from 117 to 120
Outputs:
- out: bfloat16 [4096, 4096], P(('dp', 'tensor'))
- grad_gate: bfloat16 [4096, 14336], P('dp', 'tensor')
- grad_up: bfloat16 [4096, 14336], P('dp', 'tensor')
- grad_weight: bfloat16 [14336, 4096], P('tensor', 'dp')
Inputs may be any that keep to these rules, and one draw needn't show every extreme that they name: `codes`: every entry is an FP8 E4M3 normal value (sign, exponent field 4 to 9, three mantissa bits), held exactly.
All inputs are finite; a program needn't handle non-finite values.
Results may differ from a plain program's by a relative error of at most 0.022.
Values may be sent and summed in bfloat16 or wider, within the bound.
A program may use at most 192 MiB of HBM per device.

v0:
```python
import jax
import jax.numpy as jnp
from jax import lax
from jax.sharding import PartitionSpec as P


def decode(codes, scales):
    factor = jnp.exp2(scales.astype(jnp.float32) - 127.0).astype(jnp.bfloat16)
    blocks = codes.reshape(scales.shape[0], 32, codes.shape[1]) * factor[:, None, :]
    return blocks.reshape(codes.shape)


def weight_gradient(hidden, cotangent):
    partial_grad = lax.dot_general(
        hidden, cotangent, (((0,), (0,)), ((), ())), preferred_element_type=jnp.float32
    )
    return lax.psum_scatter(
        partial_grad.astype(jnp.bfloat16), "dp", scatter_dimension=1, tiled=True
    )


def per_device(gate_pre, up_pre, grad_out, codes, scales):
    weight = decode(codes, scales)
    gate_value = gate_pre.astype(jnp.float32)
    up_value = up_pre.astype(jnp.float32)
    sigmoid_gate = jax.nn.sigmoid(gate_value)
    hidden = (gate_value * sigmoid_gate * up_value).astype(jnp.bfloat16)
    out = lax.psum_scatter(
        jnp.dot(hidden, weight, preferred_element_type=jnp.float32).astype(jnp.bfloat16),
        "tensor",
        scatter_dimension=0,
        tiled=True,
    )
    cotangent = lax.all_gather(grad_out, "tensor", axis=0, tiled=True)
    grad_hidden = lax.dot_general(
        cotangent, weight, (((1,), (1,)), ((), ())), preferred_element_type=jnp.float32
    )
    grad_weight = weight_gradient(hidden, cotangent)
    grad_gate = (
        grad_hidden * up_value * sigmoid_gate * (1.0 + gate_value * (1.0 - sigmoid_gate))
    ).astype(jnp.bfloat16)
    grad_up = (grad_hidden * gate_value * sigmoid_gate).astype(jnp.bfloat16)
    return (out, grad_gate, grad_up, grad_weight)


def solution(mesh):
    in_specs = (
        P("dp", "tensor"),
        P("dp", "tensor"),
        P(("dp", "tensor"), None),
        P("tensor", None),
        P("tensor", None),
    )
    out_specs = (P(("dp", "tensor"), None), P("dp", "tensor"), P("dp", "tensor"), P("tensor", "dp"))
    return jax.shard_map(
        per_device, mesh=mesh, in_specs=in_specs, out_specs=out_specs, check_vma=False
    )
```

profile of v0, /device:TPU:0, one launch (start us, length us, event | category | flops | bytes accessed | tf_op | source)
XLA Modules:
  0.0 361.7 jit_solution(6404392892724263409)
XLA Ops:
  7.2 0.0 all-gather.2.cloned.1.call-start
  7.2 0.7 all-gather.2.cloned.1.call-update
  7.9 0.0 copy-start
  7.9 0.0 reduce-scatter.3.cloned.1.call-start
  8.0 6.1 %copy.10 = bf16[512,3584]{0,1:T(8,128)(2,1)} copy(bf16[512,3584]{1,0:T(8,128)(2,1)} %param.6) | data formatting | bytes 7340032 | tf_op args[1]
  14.0 6.0 %copy.9 = bf16[512,3584]{0,1:T(8,128)(2,1)} copy(bf16[512,3584]{1,0:T(8,128)(2,1)} %param.5) | data formatting | bytes 7340032 | tf_op args[0]
  20.0 0.0 copy-done
  20.0 0.3 exponential_convert_fusion
  20.3 20.5 %bitcast_multiply_fusion = bf16[3584,4096]{1,0:T(8,128)(2,1)} fusion(bf16[3584,4096]{1,0:T(8,128)(2,1)} %param.8, bf16[112,4096]{1,0:T(8,128)(2,1)S(1)} %exponential_convert_fusion), kind=kLoop, calls=%fused_computation.1 | loop fusion | flops 14680064 | bytes 59637760 | tf_op jit(solution)/shard_map/mul | solution.py:9
  40.8 26.2 %convolution_convert_fusion.1 = bf16[512,4096]{1,0:T(8,128)(2,1)} fusion(bf16[3584,4096]{1,0:T(8,128)(2,1)} %bitcast_multiply_fusion, bf16[512,3584]{0,1:T(8,128)(2,1)} %copy.10, bf16[512,3584]{0,1:T(8,128)(2,1)} %copy.9), kind=kOutput, calls=%fused_computation.18 | convolution fusion | flops 15049162752 | bytes 40894464 | tf_op jit(solution)/shard_map/dot_general | solution.py:29
  67.0 0.0 reduce-scatter.3.cloned.1.call-update
  67.0 0.2 reduce-scatter.5.cloned.1.call-start
  67.2 25.8 %all-gather.2.cloned.1.call-done = bf16[512,4096]{1,0:T(8,128)(2,1)} async-done(((bf16[128,4096]{1,0:T(8,128)(2,1)}), bf16[512,4096]{1,0:T(8,128)(2,1)}) %all-gather.2.cloned.1.call-update) | async-done | bytes 4194320 | tf_op jit(solution)/shard_map/all_gather | solution.py:34
  93.1 23.1 %convolution_convert_fusion = bf16[3584,4096]{1,0:T(8,128)(2,1)} fusion(bf16[512,4096]{1,0:T(8,128)(2,1)} %all-gather.2.cloned.1.call-done, bf16[512,3584]{0,1:T(8,128)(2,1)} %copy.10, bf16[512,3584]{0,1:T(8,128)(2,1)} %copy.9), kind=kOutput, calls=%fused_computation | convolution fusion | flops 15061745664 | bytes 40894464 | tf_op jit(solution)/shard_map/dot_general | solution.py:14
  116.1 0.0 reduce-scatter.5.cloned.1.call-update
  116.2 26.1 %fusion.9 = (bf16[512,3584]{0,1:T(8,128)(2,1)}, bf16[512,3584]{0,1:T(8,128)(2,1)}) fusion(bf16[512,3584]{0,1:T(8,128)(2,1)} %copy.9, bf16[512,3584]{0,1:T(8,128)(2,1)} %copy.10, bf16[3584,4096]{1,0:T(8,128)(2,1)} %bitcast_multiply_fusion, bf16[512,4096]{1,0:T(8,128)(2,1)} %all-gather.2.cloned.1.call-done), kind=kOutput, calls=%fused_computation.17 | convolution fusion | flops 15059910656 | bytes 48234496 | tf_op jit(solution)/shard_map/dot_general | solution.py:35
  142.2 6.0 %copy.11 = bf16[512,3584]{1,0:T(8,128)(2,1)} copy(bf16[512,3584]{0,1:T(8,128)(2,1)} %get-tuple-element.9) | data formatting | bytes 7340032
  148.2 5.9 %copy.12 = bf16[512,3584]{1,0:T(8,128)(2,1)} copy(bf16[512,3584]{0,1:T(8,128)(2,1)} %get-tuple-element.8) | data formatting | bytes 7340032
  154.1 17.1 %reduce-scatter.3.cloned.1.call-done = bf16[128,4096]{1,0:T(8,128)(2,1)} async-done(((bf16[512,4096]{1,0:T(8,128)(2,1)}), bf16[128,4096]{1,0:T(8,128)(2,1)}) %reduce-scatter.3.cloned.1.call-update) | async-done | bytes 1048592 | tf_op jit(solution)/shard_map/reduce_scatter | solution.py:28
  171.2 184.0 %reduce-scatter.5.cloned.1.call-done = bf16[3584,512]{1,0:T(8,128)(2,1)} async-done(((bf16[3584,4096]{1,0:T(8,128)(2,1)}), bf16[3584,512]{1,0:T(8,128)(2,1)}) %reduce-scatter.5.cloned.1.call-update) | async-done | bytes 3670032 | tf_op jit(solution)/shard_map/reduce_scatter | solution.py:17
Async XLA Ops:
  7.2 85.9 %all-gather.2.cloned.1.call-start = ((), (), s32[]{:S(2)}) async-start(), calls=%async_computation.3 | async-start | bytes 5242880 | tf_op jit(solution)/shard_map/all_gather | solution.py:34
  7.9 12.1 %copy-start = (s32[112,4096]{1,0:T(8,128)S(1)}, s32[112,4096]{1,0:T(8,128)}, u32[]{:S(2)}) copy-start(s32[112,4096]{1,0:T(8,128)} %param.9) | copy-start | bytes 5505028
  7.9 163.3 %reduce-scatter.3.cloned.1.call-start = ((), (), s32[]{:S(2)}) async-start(), calls=%async_computation.2 | async-start | bytes 5242880 | tf_op jit(solution)/shard_map/reduce_scatter | solution.py:28
  67.0 288.2 %reduce-scatter.5.cloned.1.call-start = ((), (), s32[]{:S(2)}) async-start(), calls=%async_computation.4 | async-start | bytes 33030144 | tf_op jit(solution)/shard_map/reduce_scatter | solution.py:17
Sparse Core Ops, SparseCore 0:
  9.6 83.4 all-gather.1
  95.9 75.2 reduce-scatter.2
  175.9 179.2 reduce-scatter.4
where the time goes:
time: 362 us
  waiting for transfers between devices  228 us (63%)
  matrix products  75.3 us (21%)
  local copies, waits for them, and re-layouts  23.9 us (7%)
  other arithmetic  20.8 us (6%)
  between operations  13.8 us (4%)
    reduce_scatter x1, waiting for transfers between devices, weight_gradient(): lax.psum_scatter(partial_grad.astype(jnp.bfloat16), 'dp', scatter_dimensi...  184 us
    dot_general x1, matrix products, per_device(): jnp.dot(hidden, weight, preferred_element_type=jnp.float32)  26.2 us
    dot_general x1, matrix products, per_device(): lax.dot_general(cotangent, weight, (((1,), (1,)), ((), ())), preferred_el...  26.1 us
    all_gather x1, waiting for transfers between devices, per_device(): cotangent = lax.all_gather(grad_out, 'tensor', axis=0, tiled=True)  25.8 us
    unnamed x6, local copies, waits for them, and re-layouts  23.9 us
    dot_general x1, matrix products, weight_gradient(): lax.dot_general(hidden, cotangent, (((0,), (0,)), ((), ())), preferred_el...  23.1 us
    mul x1, other arithmetic, decode(): codes.reshape(scales.shape[0], 32, codes.shape[1]) * factor[:, None, :]  20.5 us
    reduce_scatter x1, waiting for transfers between devices, per_device(): lax.psum_scatter(jnp.dot(hidden, weight, preferred_element_type=jnp.float...  17.1 us
  transfers between devices with their start and end apart: 3, of which 3 were waited for; matrix products, arithmetic and copies ran while one was open for 33% of the time, Pallas kernels for 0%

commit v1 on v0

v1 whole, which is shorter than its diff:
```python
import functools

import jax
import jax.numpy as jnp
from jax import lax
from jax.experimental import pallas as pl
from jax.experimental.pallas import tpu as pltpu
from jax.sharding import PartitionSpec as P


def decode(codes, scales):
    factor = jnp.exp2(scales.astype(jnp.float32) - 127.0).astype(jnp.bfloat16)
    blocks = codes.reshape(scales.shape[0], 32, codes.shape[1]) * factor[:, None, :]
    return blocks.reshape(codes.shape)


def exchange(value, bits, n):
    return lax.ppermute(value, "dp", [(d, d ^ bits) for d in range(n)])


def gather_hidden(halves, n):
    blocks = {0: halves}
    for j in sorted(range(2, n, 2), key=lambda j: bin(j).count("1")):
        low, high = j & -j, 1 << (j.bit_length() - 1)
        blocks[j] = (
            exchange(blocks[j ^ low][0], low, n),
            exchange(blocks[j ^ high][1], high, n),
        )
    for j in range(1, n, 2):
        blocks[j] = tuple(exchange(half, 1, n) for half in blocks[j - 1])
    return blocks


def hidden_kernel(cut, gate_ref, up_ref, whole_ref, low_ref, high_ref):
    gate_value = gate_ref[...].astype(jnp.float32)
    value = gate_value * jax.nn.sigmoid(gate_value) * up_ref[...].astype(jnp.float32)
    value = value.astype(jnp.bfloat16)
    whole_ref[...] = value
    low_ref[...] = value[:, :cut]
    high_ref[...] = value[:, cut:]


def gated(gate_pre, up_pre, cut):
    rows, ff = gate_pre.shape
    step = 64
    widths = (ff, cut, ff - cut)
    spec = [pl.BlockSpec((step, width), lambda i: (i, 0)) for width in widths]
    return pl.pallas_call(
        functools.partial(hidden_kernel, cut),
        grid=(rows // step,),
        in_specs=[spec[0], spec[0]],
        out_specs=spec,
        out_shape=[jax.ShapeDtypeStruct((rows, width), jnp.bfloat16) for width in widths],
        compiler_params=pltpu.CompilerParams(vmem_limit_bytes=24 * 2**20),
        cost_estimate=pl.CostEstimate(
            flops=8 * rows * ff, bytes_accessed=8 * rows * ff, transcendentals=rows * ff
        ),
    )(gate_pre, up_pre)


def make_per_device(n):
    def per_device(gate_pre, up_pre, grad_out, codes, scales):
        me = lax.axis_index("dp")
        cotangent = lax.all_gather(grad_out, "tensor", axis=0, tiled=True)

        ff = gate_pre.shape[1]
        cut = max(256, ff // 512 * 256)
        gate_value = gate_pre.astype(jnp.float32)
        up_value = up_pre.astype(jnp.float32)
        sigmoid_gate = jax.nn.sigmoid(gate_value)
        hidden, low, high = gated(gate_pre, up_pre, cut)
        blocks = gather_hidden((low, high), n)

        weight = decode(codes, scales)
        out = lax.psum_scatter(
            jnp.dot(hidden, weight, preferred_element_type=jnp.float32).astype(jnp.bfloat16),
            "tensor",
            scatter_dimension=0,
            tiled=True,
        )

        width = cotangent.shape[1] // n
        columns = {}
        for j in range(n):
            part = lax.dynamic_slice_in_dim(cotangent, (me ^ j) * width, width, 1)
            columns[j] = exchange(part, j, n) if j else part

        grad_hidden = lax.dot_general(
            cotangent, weight, (((1,), (1,)), ((), ())), preferred_element_type=jnp.float32
        )
        grad_gate = (
            grad_hidden * up_value * sigmoid_gate * (1.0 + gate_value * (1.0 - sigmoid_gate))
        ).astype(jnp.bfloat16)
        grad_up = (grad_hidden * gate_value * sigmoid_gate).astype(jnp.bfloat16)

        order = sorted(range(n), key=lambda j: (bin(j >> 1).count("1"), j))
        rows = []
        for half in (0, 1):
            total = None
            for j in order:
                term = lax.dot_general(
                    blocks[j][half],
                    columns[j],
                    (((0,), (0,)), ((), ())),
                    preferred_element_type=jnp.float32,
                )
                total = term if total is None else total + term
            rows.append(total.astype(jnp.bfloat16))
        grad_weight = jnp.concatenate(rows, axis=0)
        return (out, grad_gate, grad_up, grad_weight)

    return per_device


def solution(mesh):
    in_specs = (
        P("dp", "tensor"),
        P("dp", "tensor"),
        P(("dp", "tensor"), None),
        P("tensor", None),
        P("tensor", None),
    )
    out_specs = (P(("dp", "tensor"), None), P("dp", "tensor"), P("dp", "tensor"), P("tensor", "dp"))
    return jax.shard_map(
        make_per_device(mesh.shape["dp"]),
        mesh=mesh,
        in_specs=in_specs,
        out_specs=out_specs,
        check_vma=False,
    )
```

time: 362 us -> 253 us (0.70)
  waiting for transfers between devices: 228 us -> 50.3 us
  matrix products: 75.3 us -> 111 us
  starting transfers between devices: 0.3 us -> 17.1 us
  local copies, waits for them, and re-layouts: 23.9 us -> 33.4 us
    reduce_scatter x1 -> x0, waiting for transfers between devices: 184 us -> none  [weight_gradient(): lax.psum_scatter(partial_grad.astype(jnp.bfloat16), 'dp', scatter_dimensi...]
    ppermute x0 -> x21, waiting for transfers between devices: none -> 49.6 us  [exchange(): return lax.ppermute(value, 'dp', [(d, d ^ bits) for d in range(n)])]
    dot_general x1 -> x16, matrix products: 23.1 us -> 63.1 us  [per_device(): lax.dot_general(blocks[j][half], columns[j], (((0,), (0,)), ((), ())), pr...]
    all_gather x1, waiting for transfers between devices: 25.8 us -> 0.01 us  [per_device(): cotangent = lax.all_gather(grad_out, 'tensor', axis=0, tiled=True)]
    reduce_scatter x1, waiting for transfers between devices: 17.1 us -> 0.01 us  [per_device(): lax.psum_scatter(jnp.dot(hidden, weight, preferred_element_type=jnp.float...]
    ppermute x0 -> x21, starting transfers between devices: none -> 17 us  [exchange(): return lax.ppermute(value, 'dp', [(d, d ^ bits) for d in range(n)])]
    unnamed x6 -> x20, local copies, waits for them, and re-layouts: 23.9 us -> 29.6 us
    dynamic_slice x0 -> x1, local copies, waits for them, and re-layouts: none -> 3.71 us  [per_device(): part = lax.dynamic_slice_in_dim(cotangent, (me ^ j) * width, width, 1)]
  transfers between devices with their start and end apart: 3 -> 23, of which waited for: 3 -> 6; matrix products, arithmetic and copies ran while one was open for 33% -> 64% of each run, Pallas kernels for 0% -> 1%
where the time goes in v1:
time: 253 us; the launch traced here: 252 us
  matrix products  111 us (44%)
  waiting for transfers between devices  50.3 us (20%)
  local copies, waits for them, and re-layouts  33.4 us (13%)
  other arithmetic  22.5 us (9%)
  starting transfers between devices  17.1 us (7%)
  between operations  14.2 us (6%)
  Pallas kernels  3.4 us (1%)
    dot_general x16, matrix products, per_device(): lax.dot_general(blocks[j][half], columns[j], (((0,), (0,)), ((), ())), pr...  63.1 us
    ppermute x21, waiting for transfers between devices, exchange(): return lax.ppermute(value, 'dp', [(d, d ^ bits) for d in range(n)])  49.6 us
    unnamed x20, local copies, waits for them, and re-layouts  29.6 us
    dot_general x1, matrix products, per_device(): lax.dot_general(cotangent, weight, (((1,), (1,)), ((), ())), preferred_el...  25.2 us
    dot_general x1, matrix products, per_device(): jnp.dot(hidden, weight, preferred_element_type=jnp.float32)  23.1 us
    mul x1, other arithmetic, decode(): codes.reshape(scales.shape[0], 32, codes.shape[1]) * factor[:, None, :]  20.1 us
    ppermute x21, starting transfers between devices, exchange(): return lax.ppermute(value, 'dp', [(d, d ^ bits) for d in range(n)])  17 us
  transfers between devices with their start and end apart: 23, of which 6 were waited for; matrix products, arithmetic and copies ran while one was open for 64% of the time, Pallas kernels for 1%

profile of v1, /device:TPU:0, one launch (start us, length us, event | category | flops | bytes accessed | tf_op | source)
XLA Modules:
  0.0 252.3 jit_solution(7506304453800343692)
XLA Ops:
  12.0 3.4 %shard_map.84 = (bf16[512,3584]{1,0:T(8,128)(2,1)S(1)}, bf16[512,1792]{1,0:T(8,128)(2,1)S(1)}, bf16[512,1792]{1,0:T(8,128)(2,1)}) custom-call(bf16[512,3584]{1,0:T(8,128)(2,1)S(1)} %copy-done, bf16[512,3584]{1,0:T(8,128)(2,1)S(1)} %copy-done.1), custom_call_target="tpu_custom_call" | custom-call | flops 14680064 | bytes 14680064 | tf_op jit(solution)/shard_map/pallas_call | solution.py:48
  22.6 20.1 %bitcast_multiply_fusion = bf16[3584,4096]{1,0:T(8,128)(2,1)} fusion(bf16[3584,4096]{1,0:T(8,128)(2,1)} %param.8, bf16[112,4096]{1,0:T(8,128)(2,1)S(1)} %exponential_convert_fusion), kind=kLoop, calls=%fused_computation | loop fusion | flops 14680064 | bytes 59637760 | tf_op jit(solution)/shard_map/mul | solution.py:13
  42.7 23.1 %convolution_convert_fusion = bf16[512,4096]{1,0:T(8,128)(2,1)} fusion(bf16[512,3584]{1,0:T(8,128)(2,1)} %copy-done.2, bf16[3584,4096]{1,0:T(8,128)(2,1)} %bitcast_multiply_fusion), kind=kOutput, calls=%fused_computation.14 | convolution fusion | flops 15034482688 | bytes 37224448 | tf_op jit(solution)/shard_map/dot_general | solution.py:76
  65.9 5.9 %copy.10 = bf16[512,3584]{0,1:T(8,128)(2,1)} copy(bf16[512,3584]{1,0:T(8,128)(2,1)} %gate_ref.1) | data formatting | bytes 7340032 | tf_op args[0]
  71.8 5.9 %copy.9 = bf16[512,3584]{0,1:T(8,128)(2,1)} copy(bf16[512,3584]{1,0:T(8,128)(2,1)} %up_ref.1) | data formatting | bytes 7340032 | tf_op args[1]
  79.7 23.0 %collective-permute-done.6 = bf16[512,1792]{1,0:T(8,128)(2,1)} collective-permute-done((bf16[512,1792]{1,0:T(8,128)(2,1)S(1)}, bf16[512,1792]{1,0:T(8,128)(2,1)}, u32[]{:S(2)}, u32[]{:S(2)}) %collective-permute-start.6) | collective-permute-done | bytes 1835040 | tf_op jit(solution)/shard_map/ppermute | solution.py:18
  102.8 3.7 %constant_dynamic-slice_fusion = (bf16[512,512]{1,0:T(8,128)(2,1)}, bf16[512,512]{1,0:T(8,128)(2,1)S(1)}, bf16[512,512]{1,0:T(8,128)(2,1)S(1)}, bf16[512,512]{1,...) fusion(bf16[512,4096]{1,0:T(8,128)(2,1)} %all-gather.2.cloned.1.call-done, ...), kind=kLoop, calls=%fused_computation.24 | loop fusion | bytes 7340060 | tf_op jit(solution)/shard_map/dynamic_slice | solution.py:85
  108.5 25.2 %fusion.7 = (bf16[512,3584]{0,1:T(8,128)(2,1)}, bf16[512,3584]{0,1:T(8,128)(2,1)}) fusion(bf16[512,3584]{0,1:T(8,128)(2,1)} %copy.10, bf16[512,3584]{0,1:T(8,128)(2,1)} %copy.9, bf16[3584,4096]{1,0:T(8,128)(2,1)} %bitcast_multiply_fusion, bf16[512,4096]{1,0:T(8,128)(2,1)S(1)} %copy-done.3), kind=kOutput, calls=%fused_computation.11 | convolution fusion | flops 15059910656 | bytes 48234496 | tf_op jit(solution)/shard_map/dot_general | solution.py:88
  133.8 4.5 %fusion.9 = f32[1792,512]{1,0:T(8,128)} fusion(bf16[512,1792]{1,0:T(8,128)(2,1)} %get-tuple-element.9, bf16[512,4096]{1,0:T(8,128)(2,1)S(1)} %copy-done.3, s32[]{:T(128)S(6)} %select_n.24), kind=kOutput, calls=%fused_computation.19 | convolution fusion | flops 939524096 | bytes 6029316 | tf_op jit(solution)/shard_map/dot_general | solution.py:101
  138.3 5.9 %copy.11 = bf16[512,3584]{1,0:T(8,128)(2,1)} copy(bf16[512,3584]{0,1:T(8,128)(2,1)} %get-tuple-element.15) | data formatting | bytes 7340032
  144.2 5.9 %copy.12 = bf16[512,3584]{1,0:T(8,128)(2,1)} copy(bf16[512,3584]{0,1:T(8,128)(2,1)} %get-tuple-element.14) | data formatting | bytes 7340032
  150.1 4.0 %fusion.11 = f32[1792,512]{1,0:T(8,128)} fusion(bf16[512,1792]{1,0:T(8,128)(2,1)S(1)} %get-tuple-element.8, bf16[512,4096]{1,0:T(8,128)(2,1)} %all-gather.2.cloned.1.call-done, s32[]{:T(128)S(6)} %select_n.24), kind=kOutput, calls=%fused_computation.21 | convolution fusion | flops 939524096 | bytes 6029316 | tf_op jit(solution)/shard_map/dot_general | solution.py:101
  161.7 3.8 %collective-permute-done.3 = bf16[512,512]{1,0:T(8,128)(2,1)S(1)} collective-permute-done((bf16[512,512]{1,0:T(8,128)(2,1)S(1)}, bf16[512,512]{1,0:T(8,128)(2,1)S(1)}, u32[]{:S(2)}, u32[]{:S(2)}) %collective-permute-start.3) | collective-permute-done | bytes 524320 | tf_op jit(solution)/shard_map/ppermute | solution.py:18
  172.2 4.4 %collective-permute-done.11 = bf16[512,512]{1,0:T(8,128)(2,1)S(1)} collective-permute-done((bf16[512,512]{1,0:T(8,128)(2,1)S(1)}, bf16[512,512]{1,0:T(8,128)(2,1)S(1)}, u32[]{:S(2)}, u32[]{:S(2)}) %collective-permute-start.11) | collective-permute-done | bytes 524320 | tf_op jit(solution)/shard_map/ppermute | solution.py:18
  176.5 4.5 %fusion.26 = f32[1792,512]{1,0:T(8,128)} fusion(bf16[512,1792]{1,0:T(8,128)(2,1)} %collective-permute-done.19, bf16[512,512]{1,0:T(8,128)(2,1)S(1)} %collective-permute-done.11), kind=kOutput, calls=%fused_computation.43 | convolution fusion | flops 939524096 | bytes 6029312 | tf_op jit(solution)/shard_map/dot_general | solution.py:101
  185.2 5.4 %collective-permute-done.9 = bf16[512,512]{1,0:T(8,128)(2,1)S(1)} collective-permute-done((bf16[512,512]{1,0:T(8,128)(2,1)S(1)}, bf16[512,512]{1,0:T(8,128)(2,1)S(1)}, u32[]{:S(2)}, u32[]{:S(2)}) %collective-permute-start.9) | collective-permute-done | bytes 524320 | tf_op jit(solution)/shard_map/ppermute | solution.py:18
  191.8 4.5 %fusion.25 = f32[1792,512]{1,0:T(8,128)} fusion(bf16[512,1792]{1,0:T(8,128)(2,1)} %collective-permute-done.18, bf16[512,512]{1,0:T(8,128)(2,1)S(1)} %collective-permute-done.9), kind=kOutput, calls=%fused_computation.42 | convolution fusion | flops 939524096 | bytes 6029312 | tf_op jit(solution)/shard_map/dot_general | solution.py:101
  196.8 3.1 %fusion.19 = f32[1792,512]{1,0:T(8,128)} fusion(bf16[512,1792]{1,0:T(8,128)(2,1)S(1)} %collective-permute-done.8, bf16[512,512]{1,0:T(8,128)(2,1)S(1)} %collective-permute-done.9), kind=kOutput, calls=%fused_computation.36 | convolution fusion | flops 939524096 | bytes 6029312 | tf_op jit(solution)/shard_map/dot_general | solution.py:101
  199.8 5.1 %collective-permute-done.5 = bf16[512,512]{1,0:T(8,128)(2,1)S(1)} collective-permute-done((bf16[512,512]{1,0:T(8,128)(2,1)}, bf16[512,512]{1,0:T(8,128)(2,1)S(1)}, u32[]{:S(2)}, u32[]{:S(2)}) %collective-permute-start.5) | collective-permute-done | bytes 524320 | tf_op jit(solution)/shard_map/ppermute | solution.py:18
  205.0 3.0 %fusion.23 = f32[1792,512]{1,0:T(8,128)} fusion(bf16[512,1792]{1,0:T(8,128)(2,1)S(1)} %collective-permute-done.16, bf16[512,512]{1,0:T(8,128)(2,1)S(1)} %collective-permute-done.5), kind=kOutput, calls=%fused_computation.40 | convolution fusion | flops 939524096 | bytes 6029312 | tf_op jit(solution)/shard_map/dot_general | solution.py:101
  215.1 3.3 %fusion.15 = f32[1792,512]{1,0:T(8,128)} fusion(bf16[512,1792]{1,0:T(8,128)(2,1)S(1)} %collective-permute-done, bf16[512,512]{1,0:T(8,128)(2,1)S(1)} %collective-permute-done.1), kind=kOutput, calls=%fused_computation.32 | convolution fusion | flops 939524096 | bytes 6029312 | tf_op jit(solution)/shard_map/dot_general | solution.py:101
  218.4 7.8 %collective-permute-done.13 = bf16[512,512]{1,0:T(8,128)(2,1)S(1)} collective-permute-done((bf16[512,512]{1,0:T(8,128)(2,1)S(1)}, bf16[512,512]{1,0:T(8,128)(2,1)S(1)}, u32[]{:S(2)}, u32[]{:S(2)}) %collective-permute-start.13) | collective-permute-done | bytes 524320 | tf_op jit(solution)/shard_map/ppermute | solution.py:18
  226.2 8.7 %add_convert_fusion = bf16[1792,512]{1,0:T(8,128)(2,1)S(1)} fusion(f32[1792,512]{1,0:T(8,128)} %fusion.26, f32[1792,512]{1,0:T(8,128)} %fusion.25, f32[1792,512]{1,0:T(8,128)S(1)} %fusion.24, f32[1792,512]{1,0:T(8,128)} %fusion.23, f32[1792,512]{1,0:T(8,128)S(1)} %fusion.22, f32[1792,512]{1,0:T(8,128)} %fusion.9, f32[1792,512]{1,0:T(8,128)} %fusion.21, ...), kind=kOutput, calls=%fused_computation.16 | convolution fusion | flops 946864128 | bytes 29884416 | tf_op jit(solution)/shard_map/dot_general | solution.py:101
  235.0 8.4 %add_convert_fusion.1 = bf16[1792,512]{1,0:T(8,128)(2,1)S(1)} fusion(f32[1792,512]{1,0:T(8,128)S(1)} %fusion.20, f32[1792,512]{1,0:T(8,128)} %fusion.19, f32[1792,512]{1,0:T(8,128)S(1)} %fusion.18, f32[1792,512]{1,0:T(8,128)} %fusion.17, f32[1792,512]{1,0:T(8,128)S(1)} %fusion.16, f32[1792,512]{1,0:T(8,128)} %fusion.11, f32[1792,512]{1,0:T(8,128)} %fusion.15, ...), kind=kOutput, calls=%fused_computation.17 | convolution fusion | flops 946864128 | bytes 29884416 | tf_op jit(solution)/shard_map/dot_general | solution.py:101
  (67 shorter events, 45.3 us)
Async XLA Ops:
  7.2 95.6 %all-gather.2.cloned.1.call-start = ((), (), s32[]{:S(2)}) async-start(), calls=%async_computation.2 | async-start | bytes 5242880 | tf_op jit(solution)/shard_map/all_gather | solution.py:64
  7.9 237.5 %reduce-scatter.2.cloned.1.call-start = ((), (), s32[]{:S(2)}) async-start(), calls=%async_computation.1 | async-start | bytes 5242880 | tf_op jit(solution)/shard_map/reduce_scatter | solution.py:75
  12.0 10.3 %copy-start.4 = (s32[112,4096]{1,0:T(8,128)S(1)}, s32[112,4096]{1,0:T(8,128)}, u32[]{:S(2)}) copy-start(s32[112,4096]{1,0:T(8,128)} %param.9) | copy-start | bytes 5505028
  17.3 60.5 %collective-permute-start.15 = (bf16[512,1792]{1,0:T(8,128)(2,1)}, bf16[512,1792]{1,0:T(8,128)(2,1)}, u32[]{:S(2)}, u32[]{:S(2)}) collective-permute-start(bf16[512,1792]{1,0:T(8,128)(2,1)} %get-tuple-element.9), channel_id=1, source_target_pairs={{0,8},{4,12},{8,0},{12,4},{16,24},{20,28},{24,16},{28,20},{1,9},{5... | collective-permute-start | bytes 5505032 | tf_op jit(solution)/shard_map/ppermute | solution.py:18
  20.2 59.5 %collective-permute-start.17 = (bf16[512,1792]{1,0:T(8,128)(2,1)}, bf16[512,1792]{1,0:T(8,128)(2,1)}, u32[]{:S(2)}, u32[]{:S(2)}) collective-permute-start(bf16[512,1792]{1,0:T(8,128)(2,1)} %get-tuple-element.9), channel_id=1, source_target_pairs={{0,16},{4,20},{8,24},{12,28},{16,0},{20,4},{24,8},{28,12},{1,17},{... | collective-permute-start | bytes 5505032 | tf_op jit(solution)/shard_map/ppermute | solution.py:18
  21.7 81.1 %collective-permute-start.6 = (bf16[512,1792]{1,0:T(8,128)(2,1)S(1)}, bf16[512,1792]{1,0:T(8,128)(2,1)}, u32[]{:S(2)}, u32[]{:S(2)}) collective-permute-start(bf16[512,1792]{1,0:T(8,128)(2,1)S(1)} %get-tuple-element.8), channel_id=1, source_target_pairs={{0,16},{4,20},{8,24},{12,28},{16,0},{20,4},{24,8},{28,12},{1,17},{... | collective-permute-start | bytes 5505032 | tf_op jit(solution)/shard_map/ppermute | solution.py:18
  22.2 136.1 %collective-permute-start.2 = (bf16[512,1792]{1,0:T(8,128)(2,1)S(1)}, bf16[512,1792]{1,0:T(8,128)(2,1)}, u32[]{:S(2)}, u32[]{:S(2)}) collective-permute-start(bf16[512,1792]{1,0:T(8,128)(2,1)S(1)} %get-tuple-element.8), channel_id=1, source_target_pairs={{0,8},{4,12},{8,0},{12,4},{16,24},{20,28},{24,16},{28,20},{1,9},{5... | collective-permute-start | bytes 5505032 | tf_op jit(solution)/shard_map/ppermute | solution.py:18
  77.7 83.3 %collective-permute-start.19 = (bf16[512,1792]{1,0:T(8,128)(2,1)}, bf16[512,1792]{1,0:T(8,128)(2,1)}, u32[]{:S(2)}, u32[]{:S(2)}) collective-permute-start(bf16[512,1792]{1,0:T(8,128)(2,1)} %collective-permute-done.15), channel_id=1, source_target_pairs={{0,16},{4,20},{8,24},{12,28},{16,0},{20,4},{24,8},{28,12},{1,17},{... | collective-permute-start | bytes 5505032 | tf_op jit(solution)/shard_map/ppermute | solution.py:18
  79.7 92.4 %collective-permute-start.18 = (bf16[512,1792]{1,0:T(8,128)(2,1)}, bf16[512,1792]{1,0:T(8,128)(2,1)}, u32[]{:S(2)}, u32[]{:S(2)}) collective-permute-start(bf16[512,1792]{1,0:T(8,128)(2,1)} %collective-permute-done.17), channel_id=1, source_target_pairs={{0,4},{4,0},{8,12},{12,8},{16,20},{20,16},{24,28},{28,24},{1,5},{5... | collective-permute-start | bytes 5505032 | tf_op jit(solution)/shard_map/ppermute | solution.py:18
  102.8 78.3 %collective-permute-start.10 = (bf16[512,1792]{1,0:T(8,128)(2,1)}, bf16[512,1792]{1,0:T(8,128)(2,1)}, u32[]{:S(2)}, u32[]{:S(2)}) collective-permute-start(bf16[512,1792]{1,0:T(8,128)(2,1)} %collective-permute-done.6), channel_id=1, source_target_pairs={{0,8},{4,12},{8,0},{12,4},{16,24},{20,28},{24,16},{28,20},{1,9},{5... | collective-permute-start | bytes 5505032 | tf_op jit(solution)/shard_map/ppermute | solution.py:18
  106.5 47.6 %collective-permute-start.7 = (bf16[512,512]{1,0:T(8,128)(2,1)}, bf16[512,512]{1,0:T(8,128)(2,1)S(1)}, u32[]{:S(2)}, u32[]{:S(2)}) collective-permute-start(bf16[512,512]{1,0:T(8,128)(2,1)} %get-tuple-element.19), channel_id=1, source_target_pairs={{0,16},{4,20},{8,24},{12,28},{16,0},{20,4},{24,8},{28,12},{1,17},{... | collective-permute-start | bytes 1572872 | tf_op jit(solution)/shard_map/ppermute | solution.py:18
  154.2 11.3 %collective-permute-start.3 = (bf16[512,512]{1,0:T(8,128)(2,1)S(1)}, bf16[512,512]{1,0:T(8,128)(2,1)S(1)}, u32[]{:S(2)}, u32[]{:S(2)}) collective-permute-start(bf16[512,512]{1,0:T(8,128)(2,1)S(1)} %copy-done.7), channel_id=1, source_target_pairs={{0,8},{4,12},{8,0},{12,4},{16,24},{20,28},{24,16},{28,20},{1,9},{5... | collective-permute-start | bytes 1572872 | tf_op jit(solution)/shard_map/ppermute | solution.py:18
  158.3 26.8 %collective-permute-start.16 = (bf16[512,1792]{1,0:T(8,128)(2,1)}, bf16[512,1792]{1,0:T(8,128)(2,1)S(1)}, u32[]{:S(2)}, u32[]{:S(2)}) collective-permute-start(bf16[512,1792]{1,0:T(8,128)(2,1)} %collective-permute-done.15), channel_id=1, source_target_pairs={{0,4},{4,0},{8,12},{12,8},{16,20},{20,16},{24,28},{28,24},{1,5},{5... | collective-permute-start | bytes 5505032 | tf_op jit(solution)/shard_map/ppermute | solution.py:18
  161.1 35.3 %collective-permute-start.8 = (bf16[512,1792]{1,0:T(8,128)(2,1)}, bf16[512,1792]{1,0:T(8,128)(2,1)S(1)}, u32[]{:S(2)}, u32[]{:S(2)}) collective-permute-start(bf16[512,1792]{1,0:T(8,128)(2,1)} %collective-permute-done.6), channel_id=1, source_target_pairs={{0,4},{4,0},{8,12},{12,8},{16,20},{20,16},{24,28},{28,24},{1,5},{5... | collective-permute-start | bytes 5505032 | tf_op jit(solution)/shard_map/ppermute | solution.py:18
  165.5 11.1 %collective-permute-start.11 = (bf16[512,512]{1,0:T(8,128)(2,1)S(1)}, bf16[512,512]{1,0:T(8,128)(2,1)S(1)}, u32[]{:S(2)}, u32[]{:S(2)}) collective-permute-start(bf16[512,512]{1,0:T(8,128)(2,1)S(1)} %get-tuple-element.17), channel_id=1, source_target_pairs={{0,24},{4,28},{8,16},{12,20},{16,8},{20,12},{24,0},{28,4},{1,25},{... | collective-permute-start | bytes 1572872 | tf_op jit(solution)/shard_map/ppermute | solution.py:18
  172.1 35.9 %collective-permute-start.4 = (bf16[512,1792]{1,0:T(8,128)(2,1)}, bf16[512,1792]{1,0:T(8,128)(2,1)S(1)}, u32[]{:S(2)}, u32[]{:S(2)}) collective-permute-start(bf16[512,1792]{1,0:T(8,128)(2,1)} %collective-permute-done.2), channel_id=1, source_target_pairs={{0,4},{4,0},{8,12},{12,8},{16,20},{20,16},{24,28},{28,24},{1,5},{5... | collective-permute-start | bytes 5505032 | tf_op jit(solution)/shard_map/ppermute | solution.py:18
  176.5 14.1 %collective-permute-start.9 = (bf16[512,512]{1,0:T(8,128)(2,1)S(1)}, bf16[512,512]{1,0:T(8,128)(2,1)S(1)}, u32[]{:S(2)}, u32[]{:S(2)}) collective-permute-start(bf16[512,512]{1,0:T(8,128)(2,1)S(1)} %get-tuple-element.18), channel_id=1, source_target_pairs={{0,20},{4,16},{8,28},{12,24},{16,4},{20,0},{24,12},{28,8},{1,21},{... | collective-permute-start | bytes 1572872 | tf_op jit(solution)/shard_map/ppermute | solution.py:18
  181.0 30.4 %collective-permute-start.14 = (bf16[512,1792]{1,0:T(8,128)(2,1)}, bf16[512,1792]{1,0:T(8,128)(2,1)S(1)}, u32[]{:S(2)}, u32[]{:S(2)}) collective-permute-start(bf16[512,1792]{1,0:T(8,128)(2,1)} %get-tuple-element.9), channel_id=1, source_target_pairs={{0,4},{4,0},{8,12},{12,8},{16,20},{20,16},{24,28},{28,24},{1,5},{5... | collective-permute-start | bytes 5505032 | tf_op jit(solution)/shard_map/ppermute | solution.py:18
  185.1 30.0 %collective-permute-start = (bf16[512,1792]{1,0:T(8,128)(2,1)S(1)}, bf16[512,1792]{1,0:T(8,128)(2,1)S(1)}, u32[]{:S(2)}, u32[]{:S(2)}) collective-permute-start(bf16[512,1792]{1,0:T(8,128)(2,1)S(1)} %get-tuple-element.8), channel_id=1, source_target_pairs={{0,4},{4,0},{8,12},{12,8},{16,20},{20,16},{24,28},{28,24},{1,5},{5... | collective-permute-start | bytes 5505032 | tf_op jit(solution)/shard_map/ppermute | solution.py:18
  190.6 14.3 %collective-permute-start.5 = (bf16[512,512]{1,0:T(8,128)(2,1)}, bf16[512,512]{1,0:T(8,128)(2,1)S(1)}, u32[]{:S(2)}, u32[]{:S(2)}) collective-permute-start(bf16[512,512]{1,0:T(8,128)(2,1)} %get-tuple-element.20), channel_id=1, source_target_pairs={{0,12},{4,8},{8,4},{12,0},{16,28},{20,24},{24,20},{28,16},{1,13},{... | collective-permute-start | bytes 1572872 | tf_op jit(solution)/shard_map/ppermute | solution.py:18
  196.4 22.1 %collective-permute-start.20 = (bf16[512,1792]{1,0:T(8,128)(2,1)}, bf16[512,1792]{1,0:T(8,128)(2,1)S(1)}, u32[]{:S(2)}, u32[]{:S(2)}) collective-permute-start(bf16[512,1792]{1,0:T(8,128)(2,1)} %collective-permute-done.19), channel_id=1, source_target_pairs={{0,4},{4,0},{8,12},{12,8},{16,20},{20,16},{24,28},{28,24},{1,5},{5... | collective-permute-start | bytes 5505032 | tf_op jit(solution)/shard_map/ppermute | solution.py:18
  204.9 7.2 %collective-permute-start.1 = (bf16[512,512]{1,0:T(8,128)(2,1)S(1)}, bf16[512,512]{1,0:T(8,128)(2,1)S(1)}, u32[]{:S(2)}, u32[]{:S(2)}) collective-permute-start(bf16[512,512]{1,0:T(8,128)(2,1)S(1)} %copy-done.6), channel_id=1, source_target_pairs={{0,4},{4,0},{8,12},{12,8},{16,20},{20,16},{24,28},{28,24},{1,5},{5... | collective-permute-start | bytes 1572872 | tf_op jit(solution)/shard_map/ppermute | solution.py:18
  208.0 26.9 %collective-permute-start.12 = (bf16[512,1792]{1,0:T(8,128)(2,1)}, bf16[512,1792]{1,0:T(8,128)(2,1)}, u32[]{:S(2)}, u32[]{:S(2)}) collective-permute-start(bf16[512,1792]{1,0:T(8,128)(2,1)} %collective-permute-done.10), channel_id=1, source_target_pairs={{0,4},{4,0},{8,12},{12,8},{16,20},{20,16},{24,28},{28,24},{1,5},{5... | collective-permute-start | bytes 5505032 | tf_op jit(solution)/shard_map/ppermute | solution.py:18
  211.4 14.8 %collective-permute-start.13 = (bf16[512,512]{1,0:T(8,128)(2,1)S(1)}, bf16[512,512]{1,0:T(8,128)(2,1)S(1)}, u32[]{:S(2)}, u32[]{:S(2)}) collective-permute-start(bf16[512,512]{1,0:T(8,128)(2,1)S(1)} %copy-done.5), channel_id=1, source_target_pairs={{0,28},{4,24},{8,20},{12,16},{16,12},{20,8},{24,4},{28,0},{1,29},{... | collective-permute-start | bytes 1572872 | tf_op jit(solution)/shard_map/ppermute | solution.py:18
  (7 other events, 27.6 us)
Sparse Core Ops, SparseCore 0:
  9.6 83.4 all-gather.1
  95.9 75.2 reduce-scatter.1

commit v2 on v1

--- a/solution.py
+++ b/solution.py
@@ -8,10 +8,138 @@
 from jax.sharding import PartitionSpec as P
 
 
-def decode(codes, scales):
-    factor = jnp.exp2(scales.astype(jnp.float32) - 127.0).astype(jnp.bfloat16)
-    blocks = codes.reshape(scales.shape[0], 32, codes.shape[1]) * factor[:, None, :]
-    return blocks.reshape(codes.shape)
+def decoded(codes, factor):
+    rows, columns = codes.shape
+    blocks = codes.reshape(rows // 32, 32, columns) * factor.astype(jnp.bfloat16)[:, None, :]
+    return blocks.reshape(rows, columns)
+
+
+def tile_of(extent, largest):
+    tile = largest
+    while extent % tile:
+        tile //= 2
+    return tile
+
+
+def forward_kernel(hidden_ref, codes_ref, factor_ref, out_ref):
+    weight = decoded(codes_ref[...], factor_ref[...])
+    out_ref[...] = jnp.dot(
+        hidden_ref[...], weight, preferred_element_type=jnp.float32
+    ).astype(jnp.bfloat16)
+
+
+def forward(hidden, codes, factor):
+    rows, ff = hidden.shape
+    width = codes.shape[1]
+    tile = tile_of(width, 512)
+    return pl.pallas_call(
+        forward_kernel,
+        grid=(width // tile,),
+        in_specs=[
+            pl.BlockSpec((rows, ff), lambda i: (0, 0)),
+            pl.BlockSpec((ff, tile), lambda i: (0, i)),
+            pl.BlockSpec((factor.shape[0], tile), lambda i: (0, i)),
+        ],
+        out_specs=pl.BlockSpec((rows, tile), lambda i: (0, i)),
+        out_shape=jax.ShapeDtypeStruct((rows, width), jnp.bfloat16),
+        compiler_params=pltpu.CompilerParams(vmem_limit_bytes=40 * 2**20),
+        cost_estimate=pl.CostEstimate(
+            flops=2 * rows * ff * width,
+            bytes_accessed=2 * (rows * ff + ff * width + rows * width),
+            transcendentals=0,
+        ),
+    )(hidden, codes, factor)
+
+
+def backward_kernel(cot_ref, codes_ref, factor_ref, gate_ref, up_ref, grad_gate_ref, grad_up_ref):
+    weight = decoded(codes_ref[...], factor_ref[0])
+    grad_hidden = lax.dot_general(
+        cot_ref[...], weight, (((1,), (1,)), ((), ())), preferred_element_type=jnp.float32
+    )
+    gate = gate_ref[...].astype(jnp.float32)
+    up = up_ref[...].astype(jnp.float32)
+    sigmoid = jax.nn.sigmoid(gate)
+    scaled = grad_hidden * sigmoid
+    grad_gate_ref[...] = (scaled * up * (1.0 + gate * (1.0 - sigmoid))).astype(jnp.bfloat16)
+    grad_up_ref[...] = (scaled * gate).astype(jnp.bfloat16)
+
+
+def backward(cotangent, codes, factor, gate_pre, up_pre):
+    rows, width = cotangent.shape
+    ff = codes.shape[0]
+    tile = tile_of(ff, 512)
+    factor = factor.reshape(ff // tile, tile // 32, width)
+    column = pl.BlockSpec((rows, tile), lambda i: (0, i))
+    return pl.pallas_call(
+        backward_kernel,
+        grid=(ff // tile,),
+        in_specs=[
+            pl.BlockSpec((rows, width), lambda i: (0, 0)),
+            pl.BlockSpec((tile, width), lambda i: (i, 0)),
+            pl.BlockSpec((1, tile // 32, width), lambda i: (i, 0, 0)),
+            column,
+            column,
+        ],
+        out_specs=[column, column],
+        out_shape=[jax.ShapeDtypeStruct((rows, ff), jnp.bfloat16)] * 2,
+        compiler_params=pltpu.CompilerParams(vmem_limit_bytes=40 * 2**20),
+        cost_estimate=pl.CostEstimate(
+            flops=2 * rows * ff * width,
+            bytes_accessed=2 * (4 * rows * ff + ff * width + rows * width),
+            transcendentals=rows * ff,
+        ),
+    )(cotangent, codes, factor, gate_pre, up_pre)
+
+
+def turn_kernel(cot_ref, *rest):
+    rest[-1][...] = cot_ref[...].astype(jnp.float32).T.astype(jnp.bfloat16)
+
+
+def turn(cotangent, after):
+    rows, width = cotangent.shape
+    tile = tile_of(width, 512)
+    return pl.pallas_call(
+        turn_kernel,
+        grid=(width // tile,),
+        in_specs=[pl.BlockSpec((rows, tile), lambda i: (0, i))]
+        + [pl.BlockSpec(memory_space=pl.ANY)] * len(after),
+        out_specs=pl.BlockSpec((tile, rows), lambda i: (i, 0)),
+        out_shape=jax.ShapeDtypeStruct((width, rows), jnp.bfloat16),
+        compiler_params=pltpu.CompilerParams(vmem_limit_bytes=24 * 2**20),
+        cost_estimate=pl.CostEstimate(
+            flops=0, bytes_accessed=4 * rows * width, transcendentals=0
+        ),
+    )(cotangent, *after)
+
+
+def product_kernel(n, *refs):
+    hidden, columns, out_ref = refs[:n], refs[n : 2 * n], refs[2 * n]
+    total = None
+    for h_ref, c_ref in zip(hidden, columns):
+        term = jnp.dot(c_ref[...], h_ref[...], preferred_element_type=jnp.float32)
+        total = term if total is None else total + term
+    out_ref[...] = total.T.astype(jnp.bfloat16)
+
+
+def products(hidden, columns):
+    n = len(hidden)
+    tokens, ff = hidden[0].shape
+    width = columns[0].shape[0]
+    tile = tile_of(ff, 256)
+    return pl.pallas_call(
+        functools.partial(product_kernel, n),
+        grid=(ff // tile,),
+        in_specs=[pl.BlockSpec((tokens, tile), lambda i: (0, i))] * n
+        + [pl.BlockSpec((width, tokens), lambda i: (0, 0))] * n,
+        out_specs=pl.BlockSpec((tile, width), lambda i: (i, 0)),
+        out_shape=jax.ShapeDtypeStruct((ff, width), jnp.bfloat16),
+        compiler_params=pltpu.CompilerParams(vmem_limit_bytes=40 * 2**20),
+        cost_estimate=pl.CostEstimate(
+            flops=2 * n * tokens * ff * width,
+            bytes_accessed=2 * (n * tokens * (ff + width) + ff * width),
+            transcendentals=0,
+        ),
+    )(*hidden, *columns)
 
 
 def exchange(value, bits, n):
@@ -71,42 +199,36 @@
         hidden, low, high = gated(gate_pre, up_pre, cut)
         blocks = gather_hidden((low, high), n)
 
-        weight = decode(codes, scales)
-        out = lax.psum_scatter(
-            jnp.dot(hidden, weight, preferred_element_type=jnp.float32).astype(jnp.bfloat16),
-            "tensor",
-            scatter_dimension=0,
-            tiled=True,
+        first = [half for j in range(2, n, 2) if j & (j - 1) == 0 for half in blocks[j]]
+        factor = jnp.exp2(scales.astype(jnp.float32) - 127.0)
+        partial_out = forward(hidden, codes, factor)
+        out = lax.psum_scatter(partial_out, "tensor", scatter_dimension=0, tiled=True)
+
+        width = cotangent.shape[1] // n
+        turned = turn(cotangent, [partial_out, *first])
+        pairs = []
+        for j in range(0, n, 2):
+            start = ((me ^ j) // 2) * (2 * width)
+            pair = lax.dynamic_slice_in_dim(turned, start, 2 * width, 0)
+            pairs.append(exchange(pair, j, n) if j else pair)
+        core = me % 2
+        kept = [lax.dynamic_slice_in_dim(pair, core * width, width, 0) for pair in pairs]
+        given = [lax.dynamic_slice_in_dim(pair, (1 - core) * width, width, 0) for pair in pairs]
+        taken = exchange(jnp.concatenate(given, axis=0), 1, n)
+        columns = {}
+        for m in range(n // 2):
+            columns[2 * m] = kept[m]
+            columns[2 * m + 1] = taken[m * width : (m + 1) * width]
+
+        grad_gate, grad_up = backward(cotangent, codes, factor, gate_pre, up_pre)
+
+        grad_weight = jnp.concatenate(
+            [
+                products([blocks[j][half] for j in range(n)], [columns[j] for j in range(n)])
+                for half in (0, 1)
+            ],
+            axis=0,
         )
-
-        width = cotangent.shape[1] // n
-        columns = {}
-        for j in range(n):
-            part = lax.dynamic_slice_in_dim(cotangent, (me ^ j) * width, width, 1)
-            columns[j] = exchange(part, j, n) if j else part
-
-        grad_hidden = lax.dot_general(
-            cotangent, weight, (((1,), (1,)), ((), ())), preferred_element_type=jnp.float32
-        )
-        grad_gate = (
-            grad_hidden * up_value * sigmoid_gate * (1.0 + gate_value * (1.0 - sigmoid_gate))
-        ).astype(jnp.bfloat16)
-        grad_up = (grad_hidden * gate_value * sigmoid_gate).astype(jnp.bfloat16)
-
-        order = sorted(range(n), key=lambda j: (bin(j >> 1).count("1"), j))
-        rows = []
-        for half in (0, 1):
-            total = None
-            for j in order:
-                term = lax.dot_general(
-                    blocks[j][half],
-                    columns[j],
-                    (((0,), (0,)), ((), ())),
-                    preferred_element_type=jnp.float32,
-                )
-                total = term if total is None else total + term
-            rows.append(total.astype(jnp.bfloat16))
-        grad_weight = jnp.concatenate(rows, axis=0)
         return (out, grad_gate, grad_up, grad_weight)
 
     return per_device

time: 253 us -> 259 us (1.024)
  matrix products: 111 us -> 0 us
  waiting for transfers between devices: 50.3 us -> 138 us
  Pallas kernels: 3.4 us -> 69.4 us
  other arithmetic: 22.5 us -> 2.52 us
  local copies, waits for them, and re-layouts: 33.4 us -> 21.2 us
  starting transfers between devices: 17.1 us -> 12.8 us
    dot_general x18 -> x0, matrix products: 111 us -> none  [the longest x16 63.1 us: per_device(): lax.dot_general(blocks[j][half], columns[j], (((0,), (0,)), ((), ())), pr...]
    ppermute x21 -> x18, waiting for transfers between devices: 49.6 us -> 138 us  [exchange(): return lax.ppermute(value, 'dp', [(d, d ^ bits) for d in range(n)])]
    pallas_call x0 -> x5, Pallas kernels: none -> 65.6 us  [the longest x2 22.2 us: products(): pl.pallas_call(functools.partial(product_kernel, n), grid=(ff // tile,),...]
    mul x1 -> x0, other arithmetic: 20.1 us -> none  [decode(): codes.reshape(scales.shape[0], 32, codes.shape[1]) * factor[:, None, :]]
    unnamed x20 -> x26, local copies, waits for them, and re-layouts: 29.6 us -> 15 us
    ppermute x21 -> x18, starting transfers between devices: 17 us -> 12.7 us  [exchange(): return lax.ppermute(value, 'dp', [(d, d ^ bits) for d in range(n)])]
    dynamic_slice x1 -> x5, local copies, waits for them, and re-layouts: 3.71 us -> 6 us  [the longest x3 2.61 us: per_device(): lax.dynamic_slice_in_dim(pair, core * width, width, 0)]
  transfers between devices with their start and end apart: 23 -> 20, of which waited for: 6 -> 6; matrix products, arithmetic and copies ran while one was open for 64% -> 3% of each run, Pallas kernels for 1% -> 27%
where the time goes in v2:
time: 259 us
  waiting for transfers between devices  138 us (53%)
  Pallas kernels  69.4 us (27%)
  local copies, waits for them, and re-layouts  21.2 us (8%)
  between operations  14.3 us (6%)
  starting transfers between devices  12.8 us (5%)
    ppermute x18, waiting for transfers between devices, exchange(): return lax.ppermute(value, 'dp', [(d, d ^ bits) for d in range(n)])  138 us
    pallas_call x2, Pallas kernels, products(): pl.pallas_call(functools.partial(product_kernel, n), grid=(ff // tile,),...  22.2 us
    pallas_call x1, Pallas kernels, backward(): pl.pallas_call(backward_kernel, grid=(ff // tile,), in_specs=[pl.BlockSpe...  22 us
    pallas_call x1, Pallas kernels, forward(): pl.pallas_call(forward_kernel, grid=(width // tile,), in_specs=[pl.BlockS...  19.3 us
    unnamed x26, local copies, waits for them, and re-layouts  15 us
    ppermute x18, starting transfers between devices, exchange(): return lax.ppermute(value, 'dp', [(d, d ^ bits) for d in range(n)])  12.7 us
  transfers between devices with their start and end apart: 20, of which 6 were waited for; matrix products, arithmetic and copies ran while one was open for 3% of the time, Pallas kernels for 27%

profile of v2, /device:TPU:0, one launch (start us, length us, event | category | flops | bytes accessed | tf_op | source)
XLA Modules:
  0.0 258.6 jit_solution(15900595737716220944)
XLA Ops:
  8.0 2.0 copy-done.5
  10.0 2.0 copy-done.7
  12.0 3.9 %shard_map.84 = (bf16[512,3584]{1,0:T(8,128)(2,1)S(1)}, bf16[512,1792]{1,0:T(8,128)(2,1)}, bf16[512,1792]{1,0:T(8,128)(2,1)}) custom-call(bf16[512,3584]{1,0:T(8,128)(2,1)S(1)} %copy-done.5, bf16[512,3584]{1,0:T(8,128)(2,1)S(1)} %copy-done.7), custom_call_target="tpu_custom_call" | custom-call | flops 14680064 | bytes 14680064 | tf_op jit(solution)/shard_map/pallas_call | solution.py:176
  15.9 3.0 %collective-permute-start.3 = (bf16[512,1792]{1,0:T(8,128)(2,1)}, bf16[512,1792]{1,0:T(8,128)(2,1)}, u32[]{:S(2)}, u32[]{:S(2)}) collective-permute-start(bf16[512,1792]{1,0:T(8,128)(2,1)} %get-tuple-element.12.refs_0_), channel_id=1, source_target_pairs={{0,16},{4,20},{8,24},{12,28},{16,0},{20,4},{24,8},{28,12},{1,17},{... | collective-permute-start | bytes 5505032 | tf_op jit(solution)/shard_map/ppermute | solution.py:146
  21.2 19.3 %shard_map.85.rest_0_ = bf16[512,4096]{1,0:T(8,128)(2,1)S(1)} custom-call(bf16[512,3584]{1,0:T(8,128)(2,1)S(1)} %get-tuple-element.9.hidden_ref, bf16[3584,4096]{1,0:T(8,128)(2,1)} %codes_ref.3, f32[112,4096]{1,0:T(8,128)S(1)} %multiply_exponential_fusion.factor_ref), custom_call_target="tpu_custom_call" | custom-call | flops 15032385536 | bytes 37224448 | tf_op jit(solution)/shard_map/pallas_call | solution.py:35
  40.5 2.0 copy-done
  43.8 16.2 %collective-permute-done.3.rest_3_.refs_4_ = bf16[512,1792]{1,0:T(8,128)(2,1)} collective-permute-done((bf16[512,1792]{1,0:T(8,128)(2,1)}, bf16[512,1792]{1,0:T(8,128)(2,1)}, u32[]{:S(2)}, u32[]{:S(2)}) %collective-permute-start.3) | collective-permute-done | bytes 1835040 | tf_op jit(solution)/shard_map/ppermute | solution.py:146
  60.0 39.9 %collective-permute-done.7.rest_2_.refs_2_ = bf16[512,1792]{1,0:T(8,128)(2,1)S(1)} collective-permute-done((bf16[512,1792]{1,0:T(8,128)(2,1)}, bf16[512,1792]{1,0:T(8,128)(2,1)S(1)}, u32[]{:S(2)}, u32[]{:S(2)}) %collective-permute-start.7) | collective-permute-done | bytes 1835040 | tf_op jit(solution)/shard_map/ppermute | solution.py:146
  99.9 2.7 %copy-done.1 = bf16[512,4096]{1,0:T(8,128)(2,1)S(1)} copy-done((bf16[512,4096]{1,0:T(8,128)(2,1)S(1)}, bf16[512,4096]{1,0:T(8,128)(2,1)}, u32[]{:S(2)}) %copy-start.1) | copy-done | bytes 4194328
  102.6 2.2 copy-done.3
  104.8 2.0 shard_map.87
  106.9 1.8 constant_dynamic-slice_fusion.8
  110.0 1.7 collective-permute-start.9
  111.7 1.7 collective-permute-start.11
  113.4 1.6 constant_dynamic-slice_fusion.9
  115.0 20.4 %collective-permute-done.10 = bf16[1024,512]{1,0:T(8,128)(2,1)} collective-permute-done((bf16[1024,512]{1,0:T(8,128)(2,1)}, bf16[1024,512]{1,0:T(8,128)(2,1)}, u32[]{:S(2)}, u32[]{:S(2)}) %collective-permute-start.10) | collective-permute-done | bytes 1048608 | tf_op jit(solution)/shard_map/ppermute | solution.py:146
  136.7 20.6 %collective-permute-done.11 = bf16[1024,512]{1,0:T(8,128)(2,1)} collective-permute-done((bf16[1024,512]{1,0:T(8,128)(2,1)}, bf16[1024,512]{1,0:T(8,128)(2,1)}, u32[]{:S(2)}, u32[]{:S(2)}) %collective-permute-start.11) | collective-permute-done | bytes 1048608 | tf_op jit(solution)/shard_map/ppermute | solution.py:146
  158.9 1.6 collective-permute-start.5
  162.0 39.7 %collective-permute-done.5.refs_6_ = bf16[512,1792]{1,0:T(8,128)(2,1)} collective-permute-done((bf16[512,1792]{1,0:T(8,128)(2,1)}, bf16[512,1792]{1,0:T(8,128)(2,1)}, u32[]{:S(2)}, u32[]{:S(2)}) %collective-permute-start.5) | collective-permute-done | bytes 1835040 | tf_op jit(solution)/shard_map/ppermute | solution.py:146
  203.6 1.6 copy-done.10
  205.2 22.0 %shard_map.86 = (bf16[512,3584]{1,0:T(8,128)(2,1)}, bf16[512,3584]{1,0:T(8,128)(2,1)}) custom-call(bf16[512,4096]{1,0:T(8,128)(2,1)S(1)} %copy-done.4, bf16[3584,4096]{1,0:T(8,128)(2,1)} %codes_ref.3, f32[7,16,4096]{2,1,0:T(8,128)S(1)} %bitcast.1, bf16[512,3584]{1,0:T(8,128)(2,1)S(1)} %copy-done.6, bf16[512,3584]{1,0:T(8,128)(2,1)S(1)} %copy-done.8), custom_call_target="tpu_custom_call" | custom-call | flops 15032385536 | bytes 48234496 | tf_op jit(solution)/shard_map/pallas_call | solution.py:73
  227.4 11.2 %shard_map.88 = bf16[1792,512]{1,0:T(8,128)(2,1)S(1)} custom-call(bf16[512,1792]{1,0:T(8,128)(2,1)} %get-tuple-element.12.refs_0_, bf16[512,1792]{1,0:T(8,128)(2,1)} %collective-permute-done.refs_1_, bf16[512,1792]{1,0:T(8,128)(2,1)} %collective-permute-done.1.rest_1_.refs_2_, bf16[512,1792]{1,0:T(8,128)(2,1)S(1)} %collective-permute-done.2.refs_3_, ...), custom_call_target="tpu_custom_call" | custom-call | flops 7516192768 | bytes 20709376 | tf_op jit(solution)/shard_map/pallas_call | solution.py:129
  238.6 11.0 %shard_map.89 = bf16[1792,512]{1,0:T(8,128)(2,1)S(1)} custom-call(bf16[512,1792]{1,0:T(8,128)(2,1)} %get-tuple-element.13.refs_0_, bf16[512,1792]{1,0:T(8,128)(2,1)S(1)} %collective-permute-done.13.refs_1_, bf16[512,1792]{1,0:T(8,128)(2,1)S(1)} %collective-permute-done.7.rest_2_.refs_2_, bf16[512,1792]{1,0:T(8,128)(2,1)} %collective-permute-done.14.refs_3_, ...), custom_call_target="tpu_custom_call" | custom-call | flops 7516192768 | bytes 20709376 | tf_op jit(solution)/shard_map/pallas_call | solution.py:129
  249.7 2.1 pad_maximum_fusion
  (59 shorter events, 12.1 us)
Async XLA Ops:
  7.2 92.7 %all-gather.2.cloned.1.call-start = ((), (), s32[]{:S(2)}) async-start(), calls=%async_computation.2 | async-start | bytes 5242880 | tf_op jit(solution)/shard_map/all_gather | solution.py:192
  7.9 243.9 %reduce-scatter.2.cloned.1.call-start = ((), (), s32[]{:S(2)}) async-start(), calls=%async_computation.1 | async-start | bytes 5242880 | tf_op jit(solution)/shard_map/reduce_scatter | solution.py:205
  15.9 44.1 %collective-permute-start.3 = (bf16[512,1792]{1,0:T(8,128)(2,1)}, bf16[512,1792]{1,0:T(8,128)(2,1)}, u32[]{:S(2)}, u32[]{:S(2)}) collective-permute-start(bf16[512,1792]{1,0:T(8,128)(2,1)} %get-tuple-element.12.refs_0_), channel_id=1, source_target_pairs={{0,16},{4,20},{8,24},{12,28},{16,0},{20,4},{24,8},{28,12},{1,17},{... | collective-permute-start | bytes 5505032 | tf_op jit(solution)/shard_map/ppermute | solution.py:146
  18.9 81.0 %collective-permute-start.1 = (bf16[512,1792]{1,0:T(8,128)(2,1)}, bf16[512,1792]{1,0:T(8,128)(2,1)}, u32[]{:S(2)}, u32[]{:S(2)}) collective-permute-start(bf16[512,1792]{1,0:T(8,128)(2,1)} %get-tuple-element.12.refs_0_), channel_id=1, source_target_pairs={{0,8},{4,12},{8,0},{12,4},{16,24},{20,28},{24,16},{28,20},{1,9},{5... | collective-permute-start | bytes 5505032 | tf_op jit(solution)/shard_map/ppermute | solution.py:146
  20.3 79.5 %collective-permute-start.7 = (bf16[512,1792]{1,0:T(8,128)(2,1)}, bf16[512,1792]{1,0:T(8,128)(2,1)S(1)}, u32[]{:S(2)}, u32[]{:S(2)}) collective-permute-start(bf16[512,1792]{1,0:T(8,128)(2,1)} %get-tuple-element.13.refs_0_), channel_id=1, source_target_pairs={{0,8},{4,12},{8,0},{12,4},{16,24},{20,28},{24,16},{28,20},{1,9},{5... | collective-permute-start | bytes 5505032 | tf_op jit(solution)/shard_map/ppermute | solution.py:146
  20.9 79.0 %collective-permute-start.8 = (bf16[512,1792]{1,0:T(8,128)(2,1)}, bf16[512,1792]{1,0:T(8,128)(2,1)}, u32[]{:S(2)}, u32[]{:S(2)}) collective-permute-start(bf16[512,1792]{1,0:T(8,128)(2,1)} %get-tuple-element.13.refs_0_), channel_id=1, source_target_pairs={{0,16},{4,20},{8,24},{12,28},{16,0},{20,4},{24,8},{28,12},{1,17},{... | collective-permute-start | bytes 5505032 | tf_op jit(solution)/shard_map/ppermute | solution.py:146
  109.9 25.5 %collective-permute-start.10 = (bf16[1024,512]{1,0:T(8,128)(2,1)}, bf16[1024,512]{1,0:T(8,128)(2,1)}, u32[]{:S(2)}, u32[]{:S(2)}) collective-permute-start(bf16[1024,512]{1,0:T(8,128)(2,1)} %get-tuple-element.18), channel_id=1, source_target_pairs={{0,16},{4,20},{8,24},{12,28},{16,0},{20,4},{24,8},{28,12},{1,17},{... | collective-permute-start | bytes 3145736 | tf_op jit(solution)/shard_map/ppermute | solution.py:146
  110.0 26.7 %collective-permute-start.9 = (bf16[1024,512]{1,0:T(8,128)(2,1)}, bf16[1024,512]{1,0:T(8,128)(2,1)S(1)}, u32[]{:S(2)}, u32[]{:S(2)}) collective-permute-start(bf16[1024,512]{1,0:T(8,128)(2,1)} %get-tuple-element.16), channel_id=1, source_target_pairs={{0,8},{4,12},{8,0},{12,4},{16,24},{20,28},{24,16},{28,20},{1,9},{5... | collective-permute-start | bytes 3145736 | tf_op jit(solution)/shard_map/ppermute | solution.py:146
  111.7 49.3 %collective-permute-start = (bf16[512,1792]{1,0:T(8,128)(2,1)}, bf16[512,1792]{1,0:T(8,128)(2,1)}, u32[]{:S(2)}, u32[]{:S(2)}) collective-permute-start(bf16[512,1792]{1,0:T(8,128)(2,1)} %get-tuple-element.12.refs_0_), channel_id=1, source_target_pairs={{0,4},{4,0},{8,12},{12,8},{16,20},{20,16},{24,28},{28,24},{1,5},{5... | collective-permute-start | bytes 5505032 | tf_op jit(solution)/shard_map/ppermute | solution.py:146
  111.7 45.7 %collective-permute-start.11 = (bf16[1024,512]{1,0:T(8,128)(2,1)}, bf16[1024,512]{1,0:T(8,128)(2,1)}, u32[]{:S(2)}, u32[]{:S(2)}) collective-permute-start(bf16[1024,512]{1,0:T(8,128)(2,1)} %get-tuple-element.17), channel_id=1, source_target_pairs={{0,24},{4,28},{8,16},{12,20},{16,8},{20,12},{24,0},{28,4},{1,25},{... | collective-permute-start | bytes 3145736 | tf_op jit(solution)/shard_map/ppermute | solution.py:146
  113.4 90.3 %copy-start.8 = (bf16[512,3584]{1,0:T(8,128)(2,1)S(1)}, bf16[512,3584]{1,0:T(8,128)(2,1)}, u32[]{:S(2)}) copy-start(bf16[512,3584]{1,0:T(8,128)(2,1)} %up_ref.3) | copy-start | bytes 11010052
  136.7 67.0 %copy-start.6 = (bf16[512,3584]{1,0:T(8,128)(2,1)S(1)}, bf16[512,3584]{1,0:T(8,128)(2,1)}, u32[]{:S(2)}) copy-start(bf16[512,3584]{1,0:T(8,128)(2,1)} %gate_ref.3) | copy-start | bytes 11010052
  158.7 45.0 %copy-start.4 = (bf16[512,4096]{1,0:T(8,128)(2,1)S(1)}, bf16[512,4096]{1,0:T(8,128)(2,1)}, u32[]{:S(2)}) copy-start(bf16[512,4096]{1,0:T(8,128)(2,1)} %all-gather.2.cloned.1.call-done.cot_ref) | copy-start | bytes 12582916
  158.8 44.3 %collective-permute-start.12 = (bf16[2048,512]{1,0:T(8,128)(2,1)S(1)}, bf16[2048,512]{1,0:T(8,128)(2,1)S(1)}, u32[]{:S(2)}, u32[]{:S(2)}) collective-permute-start(bf16[2048,512]{1,0:T(8,128)(2,1)S(1)} %pad_maximum_fusion.1), channel_id=1, source_target_pairs={{0,4},{4,0},{8,12},{12,8},{16,20},{20,16},{24,28},{28,24},{1,5},{5... | collective-permute-start | bytes 6291464 | tf_op jit(solution)/shard_map/ppermute | solution.py:146
  158.9 42.7 %collective-permute-start.5 = (bf16[512,1792]{1,0:T(8,128)(2,1)}, bf16[512,1792]{1,0:T(8,128)(2,1)}, u32[]{:S(2)}, u32[]{:S(2)}) collective-permute-start(bf16[512,1792]{1,0:T(8,128)(2,1)} %collective-permute-done.3.rest_3_.refs_4_), channel_id=1, source_target_pairs={{0,8},{4,12},{8,0},{12,4},{16,24},{20,28},{24,16},{28,20},{1,9},{5... | collective-permute-start | bytes 5505032 | tf_op jit(solution)/shard_map/ppermute | solution.py:146
  160.5 41.1 %collective-permute-start.4 = (bf16[512,1792]{1,0:T(8,128)(2,1)}, bf16[512,1792]{1,0:T(8,128)(2,1)}, u32[]{:S(2)}, u32[]{:S(2)}) collective-permute-start(bf16[512,1792]{1,0:T(8,128)(2,1)} %collective-permute-done.3.rest_3_.refs_4_), channel_id=1, source_target_pairs={{0,4},{4,0},{8,12},{12,8},{16,20},{20,16},{24,28},{28,24},{1,5},{5... | collective-permute-start | bytes 5505032 | tf_op jit(solution)/shard_map/ppermute | solution.py:146
  160.7 41.5 %collective-permute-start.2 = (bf16[512,1792]{1,0:T(8,128)(2,1)}, bf16[512,1792]{1,0:T(8,128)(2,1)S(1)}, u32[]{:S(2)}, u32[]{:S(2)}) collective-permute-start(bf16[512,1792]{1,0:T(8,128)(2,1)} %collective-permute-done.1.rest_1_.refs_2_), channel_id=1, source_target_pairs={{0,4},{4,0},{8,12},{12,8},{16,20},{20,16},{24,28},{28,24},{1,5},{5... | collective-permute-start | bytes 5505032 | tf_op jit(solution)/shard_map/ppermute | solution.py:146
  161.0 42.1 %collective-permute-start.16 = (bf16[512,1792]{1,0:T(8,128)(2,1)S(1)}, bf16[512,1792]{1,0:T(8,128)(2,1)S(1)}, u32[]{:S(2)}, u32[]{:S(2)}) collective-permute-start(bf16[512,1792]{1,0:T(8,128)(2,1)S(1)} %collective-permute-done.7.rest_2_.refs_2_), channel_id=1, source_target_pairs={{0,16},{4,20},{8,24},{12,28},{16,0},{20,4},{24,8},{28,12},{1,17},{... | collective-permute-start | bytes 5505032 | tf_op jit(solution)/shard_map/ppermute | solution.py:146
  201.6 25.8 %collective-permute-start.6 = (bf16[512,1792]{1,0:T(8,128)(2,1)}, bf16[512,1792]{1,0:T(8,128)(2,1)}, u32[]{:S(2)}, u32[]{:S(2)}) collective-permute-start(bf16[512,1792]{1,0:T(8,128)(2,1)} %collective-permute-done.5.refs_6_), channel_id=1, source_target_pairs={{0,4},{4,0},{8,12},{12,8},{16,20},{20,16},{24,28},{28,24},{1,5},{5... | collective-permute-start | bytes 5505032 | tf_op jit(solution)/shard_map/ppermute | solution.py:146
  201.7 37.0 %collective-permute-start.13 = (bf16[512,1792]{1,0:T(8,128)(2,1)}, bf16[512,1792]{1,0:T(8,128)(2,1)S(1)}, u32[]{:S(2)}, u32[]{:S(2)}) collective-permute-start(bf16[512,1792]{1,0:T(8,128)(2,1)} %get-tuple-element.13.refs_0_), channel_id=1, source_target_pairs={{0,4},{4,0},{8,12},{12,8},{16,20},{20,16},{24,28},{28,24},{1,5},{5... | collective-permute-start | bytes 5505032 | tf_op jit(solution)/shard_map/ppermute | solution.py:146
  202.2 36.4 %collective-permute-start.14 = (bf16[512,1792]{1,0:T(8,128)(2,1)S(1)}, bf16[512,1792]{1,0:T(8,128)(2,1)}, u32[]{:S(2)}, u32[]{:S(2)}) collective-permute-start(bf16[512,1792]{1,0:T(8,128)(2,1)S(1)} %collective-permute-done.7.rest_2_.refs_2_), channel_id=1, source_target_pairs={{0,4},{4,0},{8,12},{12,8},{16,20},{20,16},{24,28},{28,24},{1,5},{5... | collective-permute-start | bytes 5505032 | tf_op jit(solution)/shard_map/ppermute | solution.py:146
  203.1 24.2 %copy-start.12 = (bf16[512,1792]{1,0:T(8,128)(2,1)}, bf16[512,1792]{1,0:T(8,128)(2,1)S(1)}, u32[]{:S(2)}) copy-start(bf16[512,1792]{1,0:T(8,128)(2,1)S(1)} %collective-permute-done.16.refs_6_) | copy-start | bytes 5505028
  203.1 35.5 %collective-permute-start.15 = (bf16[512,1792]{1,0:T(8,128)(2,1)}, bf16[512,1792]{1,0:T(8,128)(2,1)}, u32[]{:S(2)}, u32[]{:S(2)}) collective-permute-start(bf16[512,1792]{1,0:T(8,128)(2,1)} %collective-permute-done.8.rest_4_.refs_4_), channel_id=1, source_target_pairs={{0,4},{4,0},{8,12},{12,8},{16,20},{20,16},{24,28},{28,24},{1,5},{5... | collective-permute-start | bytes 5505032 | tf_op jit(solution)/shard_map/ppermute | solution.py:146
  203.1 35.5 %collective-permute-start.17 = (bf16[512,1792]{1,0:T(8,128)(2,1)S(1)}, bf16[512,1792]{1,0:T(8,128)(2,1)}, u32[]{:S(2)}, u32[]{:S(2)}) collective-permute-start(bf16[512,1792]{1,0:T(8,128)(2,1)S(1)} %collective-permute-done.16.refs_6_), channel_id=1, source_target_pairs={{0,4},{4,0},{8,12},{12,8},{16,20},{20,16},{24,28},{28,24},{1,5},{5... | collective-permute-start | bytes 5505032 | tf_op jit(solution)/shard_map/ppermute | solution.py:146
  (9 other events, 25.7 us)
Sparse Core Ops, SparseCore 0:
  9.6 83.4 all-gather.1
  95.9 75.2 reduce-scatter.1

commit v3 on v2

--- a/solution.py
+++ b/solution.py
@@ -112,6 +112,27 @@
     )(cotangent, *after)
 
 
+def pack_kernel(n, *refs):
+    rows = refs[0].shape[0]
+    for j in range(n):
+        refs[-1][j * rows : (j + 1) * rows, :] = refs[j][...]
+
+
+def pack(parts, after):
+    n, (rows, width) = len(parts), parts[0].shape
+    return pl.pallas_call(
+        functools.partial(pack_kernel, n),
+        in_specs=[pl.BlockSpec(memory_space=pltpu.VMEM)] * n
+        + [pl.BlockSpec(memory_space=pl.ANY)] * len(after),
+        out_specs=pl.BlockSpec(memory_space=pltpu.VMEM),
+        out_shape=jax.ShapeDtypeStruct((n * rows, width), parts[0].dtype),
+        compiler_params=pltpu.CompilerParams(vmem_limit_bytes=24 * 2**20),
+        cost_estimate=pl.CostEstimate(
+            flops=0, bytes_accessed=4 * n * rows * width, transcendentals=0
+        ),
+    )(*parts, *after)
+
+
 def product_kernel(n, *refs):
     hidden, columns, out_ref = refs[:n], refs[n : 2 * n], refs[2 * n]
     total = None
@@ -214,13 +235,13 @@
         core = me % 2
         kept = [lax.dynamic_slice_in_dim(pair, core * width, width, 0) for pair in pairs]
         given = [lax.dynamic_slice_in_dim(pair, (1 - core) * width, width, 0) for pair in pairs]
-        taken = exchange(jnp.concatenate(given, axis=0), 1, n)
+        grad_gate, grad_up = backward(cotangent, codes, factor, gate_pre, up_pre)
+        second = [half for j in range(2, n, 2) if j & (j - 1) for half in blocks[j]]
+        taken = exchange(pack(given, [grad_up, *second]), 1, n)
         columns = {}
         for m in range(n // 2):
             columns[2 * m] = kept[m]
             columns[2 * m + 1] = taken[m * width : (m + 1) * width]
-
-        grad_gate, grad_up = backward(cotangent, codes, factor, gate_pre, up_pre)
 
         grad_weight = jnp.concatenate(
             [

time: 259 us -> 237 us (0.915)
  waiting for transfers between devices: 138 us -> 122 us
  local copies, waits for them, and re-layouts: 21.2 us -> 15.1 us
    ppermute x18, waiting for transfers between devices: 138 us -> 122 us  [exchange(): return lax.ppermute(value, 'dp', [(d, d ^ bits) for d in range(n)])]
    unnamed x26 -> x28, local copies, waits for them, and re-layouts: 15 us -> 12.9 us
  transfers between devices with their start and end apart: 20 -> 20, of which waited for: 6 -> 8; matrix products, arithmetic and copies ran while one was open for 3% -> 2% of each run, Pallas kernels for 27% -> 29%
where the time goes in v3:
time: 237 us; the launch traced here: 236 us
  waiting for transfers between devices  122 us (51%)
  Pallas kernels  69.4 us (29%)
  local copies, waits for them, and re-layouts  15.1 us (6%)
  between operations  14.4 us (6%)
  starting transfers between devices  12.5 us (5%)
  other arithmetic  2.38 us (1%)
    ppermute x18, waiting for transfers between devices, exchange(): return lax.ppermute(value, 'dp', [(d, d ^ bits) for d in range(n)])  122 us
    pallas_call x1, Pallas kernels, backward(): pl.pallas_call(backward_kernel, grid=(ff // tile,), in_specs=[pl.BlockSpe...  22.1 us
    pallas_call x2, Pallas kernels, products(): pl.pallas_call(functools.partial(product_kernel, n), grid=(ff // tile,),...  22.1 us
    pallas_call x1, Pallas kernels, forward(): pl.pallas_call(forward_kernel, grid=(width // tile,), in_specs=[pl.BlockS...  19.3 us
    unnamed x28, local copies, waits for them, and re-layouts  12.9 us
    ppermute x18, starting transfers between devices, exchange(): return lax.ppermute(value, 'dp', [(d, d ^ bits) for d in range(n)])  12.4 us
  transfers between devices with their start and end apart: 20, of which 8 were waited for; matrix products, arithmetic and copies ran while one was open for 2% of the time, Pallas kernels for 29%

profile of v3, /device:TPU:0, one launch (start us, length us, event | category | flops | bytes accessed | tf_op | source)
XLA Modules:
  0.0 236.1 jit_solution(17294988988322085970)
XLA Ops:
  8.0 2.0 copy-done.4
  10.0 2.0 copy-done.6
  12.0 3.8 %shard_map.84 = (bf16[512,3584]{1,0:T(8,128)(2,1)S(1)}, bf16[512,1792]{1,0:T(8,128)(2,1)}, bf16[512,1792]{1,0:T(8,128)(2,1)}) custom-call(bf16[512,3584]{1,0:T(8,128)(2,1)S(1)} %copy-done.4, bf16[512,3584]{1,0:T(8,128)(2,1)S(1)} %copy-done.6), custom_call_target="tpu_custom_call" | custom-call | flops 14680064 | bytes 14680064 | tf_op jit(solution)/shard_map/pallas_call | solution.py:197
  15.9 3.0 %collective-permute-start.3 = (bf16[512,1792]{1,0:T(8,128)(2,1)}, bf16[512,1792]{1,0:T(8,128)(2,1)}, u32[]{:S(2)}, u32[]{:S(2)}) collective-permute-start(bf16[512,1792]{1,0:T(8,128)(2,1)} %get-tuple-element.12.refs_0_), channel_id=1, source_target_pairs={{0,16},{4,20},{8,24},{12,28},{16,0},{20,4},{24,8},{28,12},{1,17},{... | collective-permute-start | bytes 5505032 | tf_op jit(solution)/shard_map/ppermute | solution.py:167
  18.8 1.5 collective-permute-start.1
  21.2 19.3 %shard_map.85.rest_0_ = bf16[512,4096]{1,0:T(8,128)(2,1)S(1)} custom-call(bf16[512,3584]{1,0:T(8,128)(2,1)S(1)} %get-tuple-element.9.hidden_ref, bf16[3584,4096]{1,0:T(8,128)(2,1)} %codes_ref.3, f32[112,4096]{1,0:T(8,128)S(1)} %multiply_exponential_fusion.factor_ref), custom_call_target="tpu_custom_call" | custom-call | flops 15032385536 | bytes 37224448 | tf_op jit(solution)/shard_map/pallas_call | solution.py:35
  40.5 2.0 copy-done
  43.8 56.0 %collective-permute-done.7.rest_2_.refs_2_ = bf16[512,1792]{1,0:T(8,128)(2,1)S(1)} collective-permute-done((bf16[512,1792]{1,0:T(8,128)(2,1)}, bf16[512,1792]{1,0:T(8,128)(2,1)S(1)}, u32[]{:S(2)}, u32[]{:S(2)}) %collective-permute-start.7) | collective-permute-done | bytes 1835040 | tf_op jit(solution)/shard_map/ppermute | solution.py:167
  100.1 1.7 collective-permute-start.5
  101.8 2.2 copy-done.1
  104.0 2.2 copy-done.2
  106.2 2.0 shard_map.87
  108.3 1.6 constant_dynamic-slice_fusion.4
  109.9 1.7 collective-permute-start.11
  113.4 22.1 %shard_map.86 = (bf16[512,3584]{1,0:T(8,128)(2,1)}, bf16[512,3584]{1,0:T(8,128)(2,1)}) custom-call(bf16[512,4096]{1,0:T(8,128)(2,1)S(1)} %copy-done.3, bf16[3584,4096]{1,0:T(8,128)(2,1)} %codes_ref.3, f32[7,16,4096]{2,1,0:T(8,128)S(1)} %bitcast.1, bf16[512,3584]{1,0:T(8,128)(2,1)S(1)} %copy-done.5, bf16[512,3584]{1,0:T(8,128)(2,1)S(1)} %copy-done.7), custom_call_target="tpu_custom_call" | custom-call | flops 15032385536 | bytes 48234496 | tf_op jit(solution)/shard_map/pallas_call | solution.py:73
  135.7 31.3 %collective-permute-done.11 = bf16[1024,512]{1,0:T(8,128)(2,1)S(1)} collective-permute-done((bf16[1024,512]{1,0:T(8,128)(2,1)}, bf16[1024,512]{1,0:T(8,128)(2,1)S(1)}, u32[]{:S(2)}, u32[]{:S(2)}) %collective-permute-start.11) | collective-permute-done | bytes 1048608 | tf_op jit(solution)/shard_map/ppermute | solution.py:167
  167.1 18.4 %collective-permute-done.10 = bf16[1024,512]{1,0:T(8,128)(2,1)S(1)} collective-permute-done((bf16[1024,512]{1,0:T(8,128)(2,1)}, bf16[1024,512]{1,0:T(8,128)(2,1)S(1)}, u32[]{:S(2)}, u32[]{:S(2)}) %collective-permute-start.10) | collective-permute-done | bytes 1048608 | tf_op jit(solution)/shard_map/ppermute | solution.py:167
  187.4 5.9 %collective-permute-done.refs_1_ = bf16[512,1792]{1,0:T(8,128)(2,1)S(1)} collective-permute-done((bf16[512,1792]{1,0:T(8,128)(2,1)}, bf16[512,1792]{1,0:T(8,128)(2,1)S(1)}, u32[]{:S(2)}, u32[]{:S(2)}) %collective-permute-start) | collective-permute-done | bytes 1835040 | tf_op jit(solution)/shard_map/ppermute | solution.py:167
  193.5 2.5 %collective-permute-done.4.refs_5_ = bf16[512,1792]{1,0:T(8,128)(2,1)S(1)} collective-permute-done((bf16[512,1792]{1,0:T(8,128)(2,1)}, bf16[512,1792]{1,0:T(8,128)(2,1)S(1)}, u32[]{:S(2)}, u32[]{:S(2)}) %collective-permute-start.4) | collective-permute-done | bytes 1835040 | tf_op jit(solution)/shard_map/ppermute | solution.py:167
  196.1 2.5 %collective-permute-done.2.refs_3_ = bf16[512,1792]{1,0:T(8,128)(2,1)S(1)} collective-permute-done((bf16[512,1792]{1,0:T(8,128)(2,1)}, bf16[512,1792]{1,0:T(8,128)(2,1)S(1)}, u32[]{:S(2)}, u32[]{:S(2)}) %collective-permute-start.2) | collective-permute-done | bytes 1835040 | tf_op jit(solution)/shard_map/ppermute | solution.py:167
  199.2 4.6 %collective-permute-done.6.refs_7_ = bf16[512,1792]{1,0:T(8,128)(2,1)S(1)} collective-permute-done((bf16[512,1792]{1,0:T(8,128)(2,1)}, bf16[512,1792]{1,0:T(8,128)(2,1)S(1)}, u32[]{:S(2)}, u32[]{:S(2)}) %collective-permute-start.6) | collective-permute-done | bytes 1835040 | tf_op jit(solution)/shard_map/ppermute | solution.py:167
  205.1 11.0 %shard_map.89 = bf16[1792,512]{1,0:T(8,128)(2,1)S(1)} custom-call(bf16[512,1792]{1,0:T(8,128)(2,1)} %get-tuple-element.12.refs_0_, bf16[512,1792]{1,0:T(8,128)(2,1)S(1)} %collective-permute-done.refs_1_, bf16[512,1792]{1,0:T(8,128)(2,1)} %collective-permute-done.1.rest_1_.refs_2_, bf16[512,1792]{1,0:T(8,128)(2,1)S(1)} %collective-permute-done.2.refs_3_, ...), custom_call_target="tpu_custom_call" | custom-call | flops 7516192768 | bytes 20709376 | tf_op jit(solution)/shard_map/pallas_call | solution.py:150
  216.1 11.1 %shard_map.90 = bf16[1792,512]{1,0:T(8,128)(2,1)S(1)} custom-call(bf16[512,1792]{1,0:T(8,128)(2,1)} %get-tuple-element.13.refs_0_, bf16[512,1792]{1,0:T(8,128)(2,1)S(1)} %collective-permute-done.14.refs_1_, bf16[512,1792]{1,0:T(8,128)(2,1)S(1)} %collective-permute-done.7.rest_2_.refs_2_, bf16[512,1792]{1,0:T(8,128)(2,1)S(1)} %collective-permute-done.15.refs_3_, ...), custom_call_target="tpu_custom_call" | custom-call | flops 7516192768 | bytes 20709376 | tf_op jit(solution)/shard_map/pallas_call | solution.py:150
  227.2 2.1 pad_maximum_fusion
  (61 shorter events, 9.4 us)
Async XLA Ops:
  7.2 94.7 %all-gather.2.cloned.1.call-start = ((), (), s32[]{:S(2)}) async-start(), calls=%async_computation.2 | async-start | bytes 5242880 | tf_op jit(solution)/shard_map/all_gather | solution.py:213
  7.9 221.4 %reduce-scatter.2.cloned.1.call-start = ((), (), s32[]{:S(2)}) async-start(), calls=%async_computation.1 | async-start | bytes 5242880 | tf_op jit(solution)/shard_map/reduce_scatter | solution.py:226
  12.0 8.8 %copy-start.11 = (s32[112,4096]{1,0:T(8,128)S(1)}, s32[112,4096]{1,0:T(8,128)}, u32[]{:S(2)}) copy-start(s32[112,4096]{1,0:T(8,128)} %param.9) | copy-start | bytes 5505028
  15.9 84.3 %collective-permute-start.3 = (bf16[512,1792]{1,0:T(8,128)(2,1)}, bf16[512,1792]{1,0:T(8,128)(2,1)}, u32[]{:S(2)}, u32[]{:S(2)}) collective-permute-start(bf16[512,1792]{1,0:T(8,128)(2,1)} %get-tuple-element.12.refs_0_), channel_id=1, source_target_pairs={{0,16},{4,20},{8,24},{12,28},{16,0},{20,4},{24,8},{28,12},{1,17},{... | collective-permute-start | bytes 5505032 | tf_op jit(solution)/shard_map/ppermute | solution.py:167
  18.8 83.0 %collective-permute-start.1 = (bf16[512,1792]{1,0:T(8,128)(2,1)}, bf16[512,1792]{1,0:T(8,128)(2,1)}, u32[]{:S(2)}, u32[]{:S(2)}) collective-permute-start(bf16[512,1792]{1,0:T(8,128)(2,1)} %get-tuple-element.12.refs_0_), channel_id=1, source_target_pairs={{0,8},{4,12},{8,0},{12,4},{16,24},{20,28},{24,16},{28,20},{1,9},{5... | collective-permute-start | bytes 5505032 | tf_op jit(solution)/shard_map/ppermute | solution.py:167
  20.3 79.5 %collective-permute-start.7 = (bf16[512,1792]{1,0:T(8,128)(2,1)}, bf16[512,1792]{1,0:T(8,128)(2,1)S(1)}, u32[]{:S(2)}, u32[]{:S(2)}) collective-permute-start(bf16[512,1792]{1,0:T(8,128)(2,1)} %get-tuple-element.13.refs_0_), channel_id=1, source_target_pairs={{0,8},{4,12},{8,0},{12,4},{16,24},{20,28},{24,16},{28,20},{1,9},{5... | collective-permute-start | bytes 5505032 | tf_op jit(solution)/shard_map/ppermute | solution.py:167
  20.8 81.0 %collective-permute-start.8 = (bf16[512,1792]{1,0:T(8,128)(2,1)}, bf16[512,1792]{1,0:T(8,128)(2,1)}, u32[]{:S(2)}, u32[]{:S(2)}) collective-permute-start(bf16[512,1792]{1,0:T(8,128)(2,1)} %get-tuple-element.13.refs_0_), channel_id=1, source_target_pairs={{0,16},{4,20},{8,24},{12,28},{16,0},{20,4},{24,8},{28,12},{1,17},{... | collective-permute-start | bytes 5505032 | tf_op jit(solution)/shard_map/ppermute | solution.py:167
  99.8 86.3 %collective-permute-start.12 = (bf16[512,1792]{1,0:T(8,128)(2,1)S(1)}, bf16[512,1792]{1,0:T(8,128)(2,1)}, u32[]{:S(2)}, u32[]{:S(2)}) collective-permute-start(bf16[512,1792]{1,0:T(8,128)(2,1)S(1)} %collective-permute-done.7.rest_2_.refs_2_), channel_id=1, source_target_pairs={{0,16},{4,20},{8,24},{12,28},{16,0},{20,4},{24,8},{28,12},{1,17},{... | collective-permute-start | bytes 5505032 | tf_op jit(solution)/shard_map/ppermute | solution.py:167
  100.1 86.0 %collective-permute-start.5 = (bf16[512,1792]{1,0:T(8,128)(2,1)}, bf16[512,1792]{1,0:T(8,128)(2,1)}, u32[]{:S(2)}, u32[]{:S(2)}) collective-permute-start(bf16[512,1792]{1,0:T(8,128)(2,1)} %collective-permute-done.3.rest_3_.refs_4_), channel_id=1, source_target_pairs={{0,8},{4,12},{8,0},{12,4},{16,24},{20,28},{24,16},{28,20},{1,9},{5... | collective-permute-start | bytes 5505032 | tf_op jit(solution)/shard_map/ppermute | solution.py:167
  106.2 7.1 %copy-start.5 = (bf16[512,3584]{1,0:T(8,128)(2,1)S(1)}, bf16[512,3584]{1,0:T(8,128)(2,1)}, u32[]{:S(2)}) copy-start(bf16[512,3584]{1,0:T(8,128)(2,1)} %gate_ref.3) | copy-start | bytes 11010052
  106.2 7.1 %copy-start.7 = (bf16[512,3584]{1,0:T(8,128)(2,1)S(1)}, bf16[512,3584]{1,0:T(8,128)(2,1)}, u32[]{:S(2)}) copy-start(bf16[512,3584]{1,0:T(8,128)(2,1)} %up_ref.3) | copy-start | bytes 11010052
  109.9 57.1 %collective-permute-start.11 = (bf16[1024,512]{1,0:T(8,128)(2,1)}, bf16[1024,512]{1,0:T(8,128)(2,1)S(1)}, u32[]{:S(2)}, u32[]{:S(2)}) collective-permute-start(bf16[1024,512]{1,0:T(8,128)(2,1)} %get-tuple-element.14), channel_id=1, source_target_pairs={{0,24},{4,28},{8,16},{12,20},{16,8},{20,12},{24,0},{28,4},{1,25},{... | collective-permute-start | bytes 3145736 | tf_op jit(solution)/shard_map/ppermute | solution.py:167
  111.6 73.9 %collective-permute-start.10 = (bf16[1024,512]{1,0:T(8,128)(2,1)}, bf16[1024,512]{1,0:T(8,128)(2,1)S(1)}, u32[]{:S(2)}, u32[]{:S(2)}) collective-permute-start(bf16[1024,512]{1,0:T(8,128)(2,1)} %get-tuple-element.15), channel_id=1, source_target_pairs={{0,16},{4,20},{8,24},{12,28},{16,0},{20,4},{24,8},{28,12},{1,17},{... | collective-permute-start | bytes 3145736 | tf_op jit(solution)/shard_map/ppermute | solution.py:167
  112.0 74.0 %collective-permute-start.9 = (bf16[1024,512]{1,0:T(8,128)(2,1)S(1)}, bf16[1024,512]{1,0:T(8,128)(2,1)S(1)}, u32[]{:S(2)}, u32[]{:S(2)}) collective-permute-start(bf16[1024,512]{1,0:T(8,128)(2,1)S(1)} %get-tuple-element.16), channel_id=1, source_target_pairs={{0,8},{4,12},{8,0},{12,4},{16,24},{20,28},{24,16},{28,20},{1,9},{5... | collective-permute-start | bytes 3145736 | tf_op jit(solution)/shard_map/ppermute | solution.py:167
  167.0 19.1 %copy-start.8 = (bf16[512,3584]{1,0:T(8,128)(2,1)S(1)}, bf16[512,3584]{1,0:T(8,128)(2,1)}, u32[]{:S(2)}) copy-start(bf16[512,3584]{1,0:T(8,128)(2,1)} %get-tuple-element.7.refs_4_) | copy-start | bytes 11010052
  186.3 12.4 %collective-permute-start.13 = (bf16[2048,512]{1,0:T(8,128)(2,1)S(1)}, bf16[2048,512]{1,0:T(8,128)(2,1)S(1)}, u32[]{:S(2)}, u32[]{:S(2)}) collective-permute-start(bf16[2048,512]{1,0:T(8,128)(2,1)S(1)} %shard_map.88), channel_id=1, source_target_pairs={{0,4},{4,0},{8,12},{12,8},{16,20},{20,16},{24,28},{28,24},{1,5},{5... | collective-permute-start | bytes 6291464 | tf_op jit(solution)/shard_map/ppermute | solution.py:167
  186.3 7.0 %collective-permute-start = (bf16[512,1792]{1,0:T(8,128)(2,1)}, bf16[512,1792]{1,0:T(8,128)(2,1)S(1)}, u32[]{:S(2)}, u32[]{:S(2)}) collective-permute-start(bf16[512,1792]{1,0:T(8,128)(2,1)} %get-tuple-element.12.refs_0_), channel_id=1, source_target_pairs={{0,4},{4,0},{8,12},{12,8},{16,20},{20,16},{24,28},{28,24},{1,5},{5... | collective-permute-start | bytes 5505032 | tf_op jit(solution)/shard_map/ppermute | solution.py:167
  186.8 9.1 %collective-permute-start.4 = (bf16[512,1792]{1,0:T(8,128)(2,1)}, bf16[512,1792]{1,0:T(8,128)(2,1)S(1)}, u32[]{:S(2)}, u32[]{:S(2)}) collective-permute-start(bf16[512,1792]{1,0:T(8,128)(2,1)} %collective-permute-done.3.rest_3_.refs_4_), channel_id=1, source_target_pairs={{0,4},{4,0},{8,12},{12,8},{16,20},{20,16},{24,28},{28,24},{1,5},{5... | collective-permute-start | bytes 5505032 | tf_op jit(solution)/shard_map/ppermute | solution.py:167
  186.9 11.7 %collective-permute-start.2 = (bf16[512,1792]{1,0:T(8,128)(2,1)}, bf16[512,1792]{1,0:T(8,128)(2,1)S(1)}, u32[]{:S(2)}, u32[]{:S(2)}) collective-permute-start(bf16[512,1792]{1,0:T(8,128)(2,1)} %collective-permute-done.1.rest_1_.refs_2_), channel_id=1, source_target_pairs={{0,4},{4,0},{8,12},{12,8},{16,20},{20,16},{24,28},{28,24},{1,5},{5... | collective-permute-start | bytes 5505032 | tf_op jit(solution)/shard_map/ppermute | solution.py:167
  187.4 16.5 %collective-permute-start.6 = (bf16[512,1792]{1,0:T(8,128)(2,1)}, bf16[512,1792]{1,0:T(8,128)(2,1)S(1)}, u32[]{:S(2)}, u32[]{:S(2)}) collective-permute-start(bf16[512,1792]{1,0:T(8,128)(2,1)} %collective-permute-done.5.refs_5_.refs_6_), channel_id=1, source_target_pairs={{0,4},{4,0},{8,12},{12,8},{16,20},{20,16},{24,28},{28,24},{1,5},{5... | collective-permute-start | bytes 5505032 | tf_op jit(solution)/shard_map/ppermute | solution.py:167
  193.3 22.8 %collective-permute-start.14 = (bf16[512,1792]{1,0:T(8,128)(2,1)}, bf16[512,1792]{1,0:T(8,128)(2,1)S(1)}, u32[]{:S(2)}, u32[]{:S(2)}) collective-permute-start(bf16[512,1792]{1,0:T(8,128)(2,1)} %get-tuple-element.13.refs_0_), channel_id=1, source_target_pairs={{0,4},{4,0},{8,12},{12,8},{16,20},{20,16},{24,28},{28,24},{1,5},{5... | collective-permute-start | bytes 5505032 | tf_op jit(solution)/shard_map/ppermute | solution.py:167
  196.0 20.2 %collective-permute-start.15 = (bf16[512,1792]{1,0:T(8,128)(2,1)S(1)}, bf16[512,1792]{1,0:T(8,128)(2,1)S(1)}, u32[]{:S(2)}, u32[]{:S(2)}) collective-permute-start(bf16[512,1792]{1,0:T(8,128)(2,1)S(1)} %collective-permute-done.7.rest_2_.refs_2_), channel_id=1, source_target_pairs={{0,4},{4,0},{8,12},{12,8},{16,20},{20,16},{24,28},{28,24},{1,5},{5... | collective-permute-start | bytes 5505032 | tf_op jit(solution)/shard_map/ppermute | solution.py:167
  198.6 17.5 %collective-permute-start.16 = (bf16[512,1792]{1,0:T(8,128)(2,1)}, bf16[512,1792]{1,0:T(8,128)(2,1)}, u32[]{:S(2)}, u32[]{:S(2)}) collective-permute-start(bf16[512,1792]{1,0:T(8,128)(2,1)} %collective-permute-done.8.rest_4_.refs_4_), channel_id=1, source_target_pairs={{0,4},{4,0},{8,12},{12,8},{16,20},{20,16},{24,28},{28,24},{1,5},{5... | collective-permute-start | bytes 5505032 | tf_op jit(solution)/shard_map/ppermute | solution.py:167
  198.7 17.4 %collective-permute-start.17 = (bf16[512,1792]{1,0:T(8,128)(2,1)}, bf16[512,1792]{1,0:T(8,128)(2,1)}, u32[]{:S(2)}, u32[]{:S(2)}) collective-permute-start(bf16[512,1792]{1,0:T(8,128)(2,1)} %collective-permute-done.12.refs_6_), channel_id=1, source_target_pairs={{0,4},{4,0},{8,12},{12,8},{16,20},{20,16},{24,28},{28,24},{1,5},{5... | collective-permute-start | bytes 5505032 | tf_op jit(solution)/shard_map/ppermute | solution.py:167
  (10 other events, 26.4 us)
Sparse Core Ops, SparseCore 0:
  9.6 83.4 all-gather.1
  95.9 75.2 reduce-scatter.1

commit v4 on v3

--- a/solution.py
+++ b/solution.py
@@ -237,7 +237,8 @@
         given = [lax.dynamic_slice_in_dim(pair, (1 - core) * width, width, 0) for pair in pairs]
         grad_gate, grad_up = backward(cotangent, codes, factor, gate_pre, up_pre)
         second = [half for j in range(2, n, 2) if j & (j - 1) for half in blocks[j]]
-        taken = exchange(pack(given, [grad_up, *second]), 1, n)
+        other = [blocks[j][0] for j in range(1, n, 2) if (j - 1) & (j - 2) == 0 or j == 1]
+        taken = exchange(pack(given, [grad_up, *second, *other]), 1, n)
         columns = {}
         for m in range(n // 2):
             columns[2 * m] = kept[m]

time: 237 us -> 241 us (1.017)
  local copies, waits for them, and re-layouts: 15.1 us -> 30 us
  waiting for transfers between devices: 122 us -> 113 us
    unnamed x28 -> x36, local copies, waits for them, and re-layouts: 12.9 us -> 23.8 us
    ppermute x18, waiting for transfers between devices: 122 us -> 112 us  [exchange(): return lax.ppermute(value, 'dp', [(d, d ^ bits) for d in range(n)])]
    dynamic_slice x3, local copies, waits for them, and re-layouts: 0.21 us -> 2.77 us  [per_device(): lax.dynamic_slice_in_dim(pair, core * width, width, 0)]
  transfers between devices with their start and end apart: 20 -> 20, of which waited for: 8 -> 8; matrix products, arithmetic and copies ran while one was open for 2% -> 4% of each run, Pallas kernels for 29% -> 29%
where the time goes in v4:
time: 241 us
  waiting for transfers between devices  113 us (47%)
  Pallas kernels  69.5 us (29%)
  local copies, waits for them, and re-layouts  30 us (12%)
  between operations  14.4 us (6%)
  starting transfers between devices  11.6 us (5%)
    ppermute x18, waiting for transfers between devices, exchange(): return lax.ppermute(value, 'dp', [(d, d ^ bits) for d in range(n)])  112 us
    unnamed x36, local copies, waits for them, and re-layouts  23.8 us
    pallas_call x2, Pallas kernels, products(): pl.pallas_call(functools.partial(product_kernel, n), grid=(ff // tile,),...  22.2 us
    pallas_call x1, Pallas kernels, backward(): pl.pallas_call(backward_kernel, grid=(ff // tile,), in_specs=[pl.BlockSpe...  22 us
    pallas_call x1, Pallas kernels, forward(): pl.pallas_call(forward_kernel, grid=(width // tile,), in_specs=[pl.BlockS...  19.3 us
    ppermute x18, starting transfers between devices, exchange(): return lax.ppermute(value, 'dp', [(d, d ^ bits) for d in range(n)])  11.5 us
  transfers between devices with their start and end apart: 20, of which 8 were waited for; matrix products, arithmetic and copies ran while one was open for 4% of the time, Pallas kernels for 29%

profile of v4, /device:TPU:0, one launch (start us, length us, event | category | flops | bytes accessed | tf_op | source)
XLA Modules:
  0.0 240.6 jit_solution(7930449228998270567)
XLA Ops:
  8.0 2.0 copy-done.5
  10.0 2.0 copy-done.7
  12.0 3.8 %shard_map.84 = (bf16[512,3584]{1,0:T(8,128)(2,1)S(1)}, bf16[512,1792]{1,0:T(8,128)(2,1)}, bf16[512,1792]{1,0:T(8,128)(2,1)}) custom-call(bf16[512,3584]{1,0:T(8,128)(2,1)S(1)} %copy-done.5, bf16[512,3584]{1,0:T(8,128)(2,1)S(1)} %copy-done.7), custom_call_target="tpu_custom_call" | custom-call | flops 14680064 | bytes 14680064 | tf_op jit(solution)/shard_map/pallas_call | solution.py:197
  15.8 3.0 %collective-permute-start.3 = (bf16[512,1792]{1,0:T(8,128)(2,1)}, bf16[512,1792]{1,0:T(8,128)(2,1)}, u32[]{:S(2)}, u32[]{:S(2)}) collective-permute-start(bf16[512,1792]{1,0:T(8,128)(2,1)} %get-tuple-element.12.refs_0_), channel_id=1, source_target_pairs={{0,16},{4,20},{8,24},{12,28},{16,0},{20,4},{24,8},{28,12},{1,17},{... | collective-permute-start | bytes 5505032 | tf_op jit(solution)/shard_map/ppermute | solution.py:167
  21.2 19.3 %shard_map.85.rest_0_ = bf16[512,4096]{1,0:T(8,128)(2,1)S(1)} custom-call(bf16[512,3584]{1,0:T(8,128)(2,1)S(1)} %get-tuple-element.9.hidden_ref, bf16[3584,4096]{1,0:T(8,128)(2,1)} %codes_ref.3, f32[112,4096]{1,0:T(8,128)S(1)} %multiply_exponential_fusion.factor_ref), custom_call_target="tpu_custom_call" | custom-call | flops 15032385536 | bytes 37224448 | tf_op jit(solution)/shard_map/pallas_call | solution.py:35
  40.5 2.0 copy-done
  43.8 16.2 %collective-permute-done.3.rest_3_.refs_4_ = bf16[512,1792]{1,0:T(8,128)(2,1)} collective-permute-done((bf16[512,1792]{1,0:T(8,128)(2,1)}, bf16[512,1792]{1,0:T(8,128)(2,1)}, u32[]{:S(2)}, u32[]{:S(2)}) %collective-permute-start.3) | collective-permute-done | bytes 1835040 | tf_op jit(solution)/shard_map/ppermute | solution.py:167
  60.0 39.9 %collective-permute-done.7.rest_2_.refs_2_ = bf16[512,1792]{1,0:T(8,128)(2,1)S(1)} collective-permute-done((bf16[512,1792]{1,0:T(8,128)(2,1)}, bf16[512,1792]{1,0:T(8,128)(2,1)S(1)}, u32[]{:S(2)}, u32[]{:S(2)}) %collective-permute-start.7) | collective-permute-done | bytes 1835040 | tf_op jit(solution)/shard_map/ppermute | solution.py:167
  99.8 2.8 %copy-done.1 = bf16[512,4096]{1,0:T(8,128)(2,1)S(1)} copy-done((bf16[512,4096]{1,0:T(8,128)(2,1)S(1)}, bf16[512,4096]{1,0:T(8,128)(2,1)}, u32[]{:S(2)}) %copy-start.1) | copy-done | bytes 4194328
  102.6 2.2 copy-done.3
  104.8 2.0 shard_map.87
  111.0 1.9 collective-permute-start.10
  113.5 23.6 %collective-permute-done.11 = bf16[1024,512]{1,0:T(8,128)(2,1)S(1)} collective-permute-done((bf16[1024,512]{1,0:T(8,128)(2,1)}, bf16[1024,512]{1,0:T(8,128)(2,1)S(1)}, u32[]{:S(2)}, u32[]{:S(2)}) %collective-permute-start.11) | collective-permute-done | bytes 1048608 | tf_op jit(solution)/shard_map/ppermute | solution.py:167
  138.7 18.5 %collective-permute-done.10 = bf16[1024,512]{1,0:T(8,128)(2,1)} collective-permute-done((bf16[1024,512]{1,0:T(8,128)(2,1)}, bf16[1024,512]{1,0:T(8,128)(2,1)}, u32[]{:S(2)}, u32[]{:S(2)}) %collective-permute-start.10) | collective-permute-done | bytes 1048608 | tf_op jit(solution)/shard_map/ppermute | solution.py:167
  159.9 2.2 copy-done.4
  162.1 2.0 copy-done.6
  164.1 2.1 copy-done.8
  166.2 22.0 %shard_map.86 = (bf16[512,3584]{1,0:T(8,128)(2,1)}, bf16[512,3584]{1,0:T(8,128)(2,1)}) custom-call(bf16[512,4096]{1,0:T(8,128)(2,1)S(1)} %copy-done.4, bf16[3584,4096]{1,0:T(8,128)(2,1)} %codes_ref.3, f32[7,16,4096]{2,1,0:T(8,128)S(1)} %bitcast.1, bf16[512,3584]{1,0:T(8,128)(2,1)S(1)} %copy-done.6, bf16[512,3584]{1,0:T(8,128)(2,1)S(1)} %copy-done.8), custom_call_target="tpu_custom_call" | custom-call | flops 15032385536 | bytes 48234496 | tf_op jit(solution)/shard_map/pallas_call | solution.py:73
  191.0 5.3 %collective-permute-done.12.refs_6_ = bf16[512,1792]{1,0:T(8,128)(2,1)S(1)} collective-permute-done((bf16[512,1792]{1,0:T(8,128)(2,1)S(1)}, bf16[512,1792]{1,0:T(8,128)(2,1)S(1)}, u32[]{:S(2)}, u32[]{:S(2)}) %collective-permute-start.12) | collective-permute-done | bytes 1835040 | tf_op jit(solution)/shard_map/ppermute | solution.py:167
  199.2 2.6 %collective-permute-done.13 = bf16[2048,512]{1,0:T(8,128)(2,1)S(1)} collective-permute-done((bf16[2048,512]{1,0:T(8,128)(2,1)S(1)}, bf16[2048,512]{1,0:T(8,128)(2,1)S(1)}, u32[]{:S(2)}, u32[]{:S(2)}) %collective-permute-start.13) | collective-permute-done | bytes 2097184 | tf_op jit(solution)/shard_map/ppermute | solution.py:167
  202.1 5.0 %collective-permute-done.6.refs_7_ = bf16[512,1792]{1,0:T(8,128)(2,1)S(1)} collective-permute-done((bf16[512,1792]{1,0:T(8,128)(2,1)S(1)}, bf16[512,1792]{1,0:T(8,128)(2,1)S(1)}, u32[]{:S(2)}, u32[]{:S(2)}) %collective-permute-start.6) | collective-permute-done | bytes 1835040 | tf_op jit(solution)/shard_map/ppermute | solution.py:167
  208.3 11.1 %shard_map.89 = bf16[1792,512]{1,0:T(8,128)(2,1)S(1)} custom-call(bf16[512,1792]{1,0:T(8,128)(2,1)} %get-tuple-element.12.refs_0_, bf16[512,1792]{1,0:T(8,128)(2,1)} %collective-permute-done.refs_7_.refs_1_, bf16[512,1792]{1,0:T(8,128)(2,1)} %collective-permute-done.1.rest_1_.refs_2_, bf16[512,1792]{1,0:T(8,128)(2,1)S(1)} %collective-permute-done.2.refs_8_.refs_3_, ...), custom_call_target="tpu_custom_call" | custom-call | flops 7516192768 | bytes 20709376 | tf_op jit(solution)/shard_map/pallas_call | solution.py:150
  220.7 11.0 %shard_map.90 = bf16[1792,512]{1,0:T(8,128)(2,1)S(1)} custom-call(bf16[512,1792]{1,0:T(8,128)(2,1)} %get-tuple-element.13.refs_0_, bf16[512,1792]{1,0:T(8,128)(2,1)S(1)} %collective-permute-done.14.refs_1_, bf16[512,1792]{1,0:T(8,128)(2,1)S(1)} %collective-permute-done.7.rest_2_.refs_2_, bf16[512,1792]{1,0:T(8,128)(2,1)S(1)} %collective-permute-done.15.refs_3_, ...), custom_call_target="tpu_custom_call" | custom-call | flops 7516192768 | bytes 20709376 | tf_op jit(solution)/shard_map/pallas_call | solution.py:150
  231.7 2.1 pad_maximum_fusion
  (69 shorter events, 21.8 us)
Async XLA Ops:
  7.2 92.7 %all-gather.2.cloned.1.call-start = ((), (), s32[]{:S(2)}) async-start(), calls=%async_computation.2 | async-start | bytes 5242880 | tf_op jit(solution)/shard_map/all_gather | solution.py:213
  7.9 225.9 %reduce-scatter.2.cloned.1.call-start = ((), (), s32[]{:S(2)}) async-start(), calls=%async_computation.1 | async-start | bytes 5242880 | tf_op jit(solution)/shard_map/reduce_scatter | solution.py:226
  12.0 8.8 %copy-start.15 = (s32[112,4096]{1,0:T(8,128)S(1)}, s32[112,4096]{1,0:T(8,128)}, u32[]{:S(2)}) copy-start(s32[112,4096]{1,0:T(8,128)} %param.9) | copy-start | bytes 5505028
  15.8 44.1 %collective-permute-start.3 = (bf16[512,1792]{1,0:T(8,128)(2,1)}, bf16[512,1792]{1,0:T(8,128)(2,1)}, u32[]{:S(2)}, u32[]{:S(2)}) collective-permute-start(bf16[512,1792]{1,0:T(8,128)(2,1)} %get-tuple-element.12.refs_0_), channel_id=1, source_target_pairs={{0,16},{4,20},{8,24},{12,28},{16,0},{20,4},{24,8},{28,12},{1,17},{... | collective-permute-start | bytes 5505032 | tf_op jit(solution)/shard_map/ppermute | solution.py:167
  18.8 81.0 %collective-permute-start.1 = (bf16[512,1792]{1,0:T(8,128)(2,1)}, bf16[512,1792]{1,0:T(8,128)(2,1)}, u32[]{:S(2)}, u32[]{:S(2)}) collective-permute-start(bf16[512,1792]{1,0:T(8,128)(2,1)} %get-tuple-element.12.refs_0_), channel_id=1, source_target_pairs={{0,8},{4,12},{8,0},{12,4},{16,24},{20,28},{24,16},{28,20},{1,9},{5... | collective-permute-start | bytes 5505032 | tf_op jit(solution)/shard_map/ppermute | solution.py:167
  20.3 79.5 %collective-permute-start.7 = (bf16[512,1792]{1,0:T(8,128)(2,1)}, bf16[512,1792]{1,0:T(8,128)(2,1)S(1)}, u32[]{:S(2)}, u32[]{:S(2)}) collective-permute-start(bf16[512,1792]{1,0:T(8,128)(2,1)} %get-tuple-element.13.refs_0_), channel_id=1, source_target_pairs={{0,8},{4,12},{8,0},{12,4},{16,24},{20,28},{24,16},{28,20},{1,9},{5... | collective-permute-start | bytes 5505032 | tf_op jit(solution)/shard_map/ppermute | solution.py:167
  20.8 79.0 %collective-permute-start.8 = (bf16[512,1792]{1,0:T(8,128)(2,1)}, bf16[512,1792]{1,0:T(8,128)(2,1)}, u32[]{:S(2)}, u32[]{:S(2)}) collective-permute-start(bf16[512,1792]{1,0:T(8,128)(2,1)} %get-tuple-element.13.refs_0_), channel_id=1, source_target_pairs={{0,16},{4,20},{8,24},{12,28},{16,0},{20,4},{24,8},{28,12},{1,17},{... | collective-permute-start | bytes 5505032 | tf_op jit(solution)/shard_map/ppermute | solution.py:167
  109.8 27.2 %collective-permute-start.11 = (bf16[1024,512]{1,0:T(8,128)(2,1)}, bf16[1024,512]{1,0:T(8,128)(2,1)S(1)}, u32[]{:S(2)}, u32[]{:S(2)}) collective-permute-start(bf16[1024,512]{1,0:T(8,128)(2,1)} %get-tuple-element.14), channel_id=1, source_target_pairs={{0,24},{4,28},{8,16},{12,20},{16,8},{20,12},{24,0},{28,4},{1,25},{... | collective-permute-start | bytes 3145736 | tf_op jit(solution)/shard_map/ppermute | solution.py:167
  111.0 46.1 %collective-permute-start.10 = (bf16[1024,512]{1,0:T(8,128)(2,1)}, bf16[1024,512]{1,0:T(8,128)(2,1)}, u32[]{:S(2)}, u32[]{:S(2)}) collective-permute-start(bf16[1024,512]{1,0:T(8,128)(2,1)} %get-tuple-element.15), channel_id=1, source_target_pairs={{0,16},{4,20},{8,24},{12,28},{16,0},{20,4},{24,8},{28,12},{1,17},{... | collective-permute-start | bytes 3145736 | tf_op jit(solution)/shard_map/ppermute | solution.py:167
  112.9 45.4 %collective-permute-start.9 = (bf16[1024,512]{1,0:T(8,128)(2,1)}, bf16[1024,512]{1,0:T(8,128)(2,1)}, u32[]{:S(2)}, u32[]{:S(2)}) collective-permute-start(bf16[1024,512]{1,0:T(8,128)(2,1)} %get-tuple-element.16), channel_id=1, source_target_pairs={{0,8},{4,12},{8,0},{12,4},{16,24},{20,28},{24,16},{28,20},{1,9},{5... | collective-permute-start | bytes 3145736 | tf_op jit(solution)/shard_map/ppermute | solution.py:167
  113.3 77.7 %collective-permute-start = (bf16[512,1792]{1,0:T(8,128)(2,1)}, bf16[512,1792]{1,0:T(8,128)(2,1)}, u32[]{:S(2)}, u32[]{:S(2)}) collective-permute-start(bf16[512,1792]{1,0:T(8,128)(2,1)} %get-tuple-element.12.refs_0_), channel_id=1, source_target_pairs={{0,4},{4,0},{8,12},{12,8},{16,20},{20,16},{24,28},{28,24},{1,5},{5... | collective-permute-start | bytes 5505032 | tf_op jit(solution)/shard_map/ppermute | solution.py:167
  113.3 46.5 %copy-start.14 = (f32[112,4096]{1,0:T(8,128)S(1)}, f32[112,4096]{1,0:T(8,128)}, u32[]{:S(2)}) copy-start(f32[112,4096]{1,0:T(8,128)} %copy-done.13) | copy-start | bytes 5505028
  113.3 82.9 %collective-permute-start.12 = (bf16[512,1792]{1,0:T(8,128)(2,1)S(1)}, bf16[512,1792]{1,0:T(8,128)(2,1)S(1)}, u32[]{:S(2)}, u32[]{:S(2)}) collective-permute-start(bf16[512,1792]{1,0:T(8,128)(2,1)S(1)} %collective-permute-done.7.rest_2_.refs_2_), channel_id=1, source_target_pairs={{0,16},{4,20},{8,24},{12,28},{16,0},{20,4},{24,8},{28,12},{1,17},{... | collective-permute-start | bytes 5505032 | tf_op jit(solution)/shard_map/ppermute | solution.py:167
  137.1 59.2 %collective-permute-start.5 = (bf16[512,1792]{1,0:T(8,128)(2,1)}, bf16[512,1792]{1,0:T(8,128)(2,1)S(1)}, u32[]{:S(2)}, u32[]{:S(2)}) collective-permute-start(bf16[512,1792]{1,0:T(8,128)(2,1)} %collective-permute-done.3.rest_3_.refs_4_), channel_id=1, source_target_pairs={{0,8},{4,12},{8,0},{12,4},{16,24},{20,28},{24,16},{28,20},{1,9},{5... | collective-permute-start | bytes 5505032 | tf_op jit(solution)/shard_map/ppermute | solution.py:167
  157.2 39.1 %collective-permute-start.4 = (bf16[512,1792]{1,0:T(8,128)(2,1)}, bf16[512,1792]{1,0:T(8,128)(2,1)S(1)}, u32[]{:S(2)}, u32[]{:S(2)}) collective-permute-start(bf16[512,1792]{1,0:T(8,128)(2,1)} %collective-permute-done.3.rest_3_.refs_4_), channel_id=1, source_target_pairs={{0,4},{4,0},{8,12},{12,8},{16,20},{20,16},{24,28},{28,24},{1,5},{5... | collective-permute-start | bytes 5505032 | tf_op jit(solution)/shard_map/ppermute | solution.py:167
  158.4 37.9 %collective-permute-start.2 = (bf16[512,1792]{1,0:T(8,128)(2,1)}, bf16[512,1792]{1,0:T(8,128)(2,1)S(1)}, u32[]{:S(2)}, u32[]{:S(2)}) collective-permute-start(bf16[512,1792]{1,0:T(8,128)(2,1)} %collective-permute-done.1.rest_1_.refs_2_), channel_id=1, source_target_pairs={{0,4},{4,0},{8,12},{12,8},{16,20},{20,16},{24,28},{28,24},{1,5},{5... | collective-permute-start | bytes 5505032 | tf_op jit(solution)/shard_map/ppermute | solution.py:167
  188.3 8.0 %copy-start.9 = (bf16[512,3584]{1,0:T(8,128)(2,1)S(1)}, bf16[512,3584]{1,0:T(8,128)(2,1)}, u32[]{:S(2)}) copy-start(bf16[512,3584]{1,0:T(8,128)(2,1)} %get-tuple-element.7.refs_4_) | copy-start | bytes 11010052
  196.3 5.5 %copy-start.10 = (bf16[512,1792]{1,0:T(8,128)(2,1)}, bf16[512,1792]{1,0:T(8,128)(2,1)S(1)}, u32[]{:S(2)}) copy-start(bf16[512,1792]{1,0:T(8,128)(2,1)S(1)} %collective-permute-done.12.refs_6_) | copy-start | bytes 5505028
  197.6 4.2 %collective-permute-start.13 = (bf16[2048,512]{1,0:T(8,128)(2,1)S(1)}, bf16[2048,512]{1,0:T(8,128)(2,1)S(1)}, u32[]{:S(2)}, u32[]{:S(2)}) collective-permute-start(bf16[2048,512]{1,0:T(8,128)(2,1)S(1)} %shard_map.88), channel_id=1, source_target_pairs={{0,4},{4,0},{8,12},{12,8},{16,20},{20,16},{24,28},{28,24},{1,5},{5... | collective-permute-start | bytes 6291464 | tf_op jit(solution)/shard_map/ppermute | solution.py:167
  198.1 8.9 %collective-permute-start.6 = (bf16[512,1792]{1,0:T(8,128)(2,1)S(1)}, bf16[512,1792]{1,0:T(8,128)(2,1)S(1)}, u32[]{:S(2)}, u32[]{:S(2)}) collective-permute-start(bf16[512,1792]{1,0:T(8,128)(2,1)S(1)} %collective-permute-done.5.refs_5_.refs_6_), channel_id=1, source_target_pairs={{0,4},{4,0},{8,12},{12,8},{16,20},{20,16},{24,28},{28,24},{1,5},{5... | collective-permute-start | bytes 5505032 | tf_op jit(solution)/shard_map/ppermute | solution.py:167
  198.1 21.3 %collective-permute-start.14 = (bf16[512,1792]{1,0:T(8,128)(2,1)}, bf16[512,1792]{1,0:T(8,128)(2,1)S(1)}, u32[]{:S(2)}, u32[]{:S(2)}) collective-permute-start(bf16[512,1792]{1,0:T(8,128)(2,1)} %get-tuple-element.13.refs_0_), channel_id=1, source_target_pairs={{0,4},{4,0},{8,12},{12,8},{16,20},{20,16},{24,28},{28,24},{1,5},{5... | collective-permute-start | bytes 5505032 | tf_op jit(solution)/shard_map/ppermute | solution.py:167
  198.6 20.8 %collective-permute-start.15 = (bf16[512,1792]{1,0:T(8,128)(2,1)S(1)}, bf16[512,1792]{1,0:T(8,128)(2,1)S(1)}, u32[]{:S(2)}, u32[]{:S(2)}) collective-permute-start(bf16[512,1792]{1,0:T(8,128)(2,1)S(1)} %collective-permute-done.7.rest_2_.refs_2_), channel_id=1, source_target_pairs={{0,4},{4,0},{8,12},{12,8},{16,20},{20,16},{24,28},{28,24},{1,5},{5... | collective-permute-start | bytes 5505032 | tf_op jit(solution)/shard_map/ppermute | solution.py:167
  198.7 20.8 %collective-permute-start.16 = (bf16[512,1792]{1,0:T(8,128)(2,1)}, bf16[512,1792]{1,0:T(8,128)(2,1)S(1)}, u32[]{:S(2)}, u32[]{:S(2)}) collective-permute-start(bf16[512,1792]{1,0:T(8,128)(2,1)} %collective-permute-done.8.rest_4_.refs_4_), channel_id=1, source_target_pairs={{0,4},{4,0},{8,12},{12,8},{16,20},{20,16},{24,28},{28,24},{1,5},{5... | collective-permute-start | bytes 5505032 | tf_op jit(solution)/shard_map/ppermute | solution.py:167
  201.8 17.7 %collective-permute-start.17 = (bf16[512,1792]{1,0:T(8,128)(2,1)S(1)}, bf16[512,1792]{1,0:T(8,128)(2,1)}, u32[]{:S(2)}, u32[]{:S(2)}) collective-permute-start(bf16[512,1792]{1,0:T(8,128)(2,1)S(1)} %collective-permute-done.12.refs_6_), channel_id=1, source_target_pairs={{0,4},{4,0},{8,12},{12,8},{16,20},{20,16},{24,28},{28,24},{1,5},{5... | collective-permute-start | bytes 5505032 | tf_op jit(solution)/shard_map/ppermute | solution.py:167
  (14 other events, 27.2 us)
Sparse Core Ops, SparseCore 0:
  9.6 83.4 all-gather.1
  95.9 75.2 reduce-scatter.1
